TPU v7x, 768 devices: a whole 4x8x12 slice. The times are simulated.
768 devices in a mesh: dom: 96 (over x, z, core), feat: 8 (over y).
Axes of the slice: x: 4, y: 8, z: 12, core: 2. Of those that a mesh axis runs over, the one named last changes fastest.
Arguments:
- features: bfloat16 [49152, 256], P('dom', 'feat'), may hold values from -6 to 6
- weight: bfloat16 [512, 256], P(None, 'feat'), may hold values from -0.25 to 0.25
- bias: bfloat16 [256], P('feat'), may hold values from -3 to 3
- local_src: int32 [196608], P('dom'), may hold values from 0 to 511
- local_dst: int32 [196608], P('dom'), may hold values from 0 to 511
- hub_rows: int32 [1536], P('dom'), may hold values from 0 to 511
- hub_src: int32 [98304], P('dom'), may hold values from 0 to 1535
- hub_dst: int32 [98304], P('dom'), may hold values from 0 to 511
- send_rows: int32 [9216, 8], P('dom'), may hold values from 0 to 511
- bnd_src: int32 [98304], P('dom'), may hold values from 0 to 767
- bnd_dst: int32 [98304], P('dom'), may hold values from 0 to 511
Outputs:
- hidden: bfloat16 [49152, 256], P('dom', 'feat')
All inputs are finite; a program needn't handle non-finite values.
Results may differ from a plain program's by a relative error of at most 0.0027.
Values may be sent and summed in bfloat16 or wider, within the bound.
A program may use at most 32 MiB of HBM per device.

v0:
```python
import jax
import jax.numpy as jnp
from jax import lax
from jax.sharding import PartitionSpec as P


def pool_rows(table, source, target, count):
    return jax.ops.segment_sum(
        jnp.take(table, source, axis=0).astype(jnp.float32), target, num_segments=count
    )


def count_edges(target, count):
    return jax.ops.segment_sum(jnp.ones(target.shape, jnp.float32), target, num_segments=count)


def shards(
    features,
    weight,
    bias,
    local_src,
    local_dst,
    hub_rows,
    hub_src,
    hub_dst,
    send_rows,
    bnd_src,
    bnd_dst,
):
    count = features.shape[0]
    width = features.shape[1]
    full_width = weight.shape[0] // 2
    hub_local = jnp.take(features, hub_rows, axis=0)
    hub_table = lax.all_gather(hub_local, "dom", axis=0, tiled=True)
    outgoing = jnp.take(features, send_rows, axis=0)
    incoming = lax.all_to_all(outgoing, "dom", split_axis=0, concat_axis=0, tiled=True)
    received = incoming.reshape(incoming.shape[0] * incoming.shape[1], width)
    pooled = pool_rows(features, local_src, local_dst, count)
    degree = (
        count_edges(local_dst, count) + count_edges(hub_dst, count) + count_edges(bnd_dst, count)
    )
    pooled = pooled + pool_rows(hub_table, hub_src, hub_dst, count)
    pooled = pooled + pool_rows(received, bnd_src, bnd_dst, count)
    neighbour = (pooled / jnp.maximum(degree, 1.0)[:, None]).astype(jnp.bfloat16)
    whole_self, whole_pool = (
        lax.all_gather(features, "feat", axis=1, tiled=True),
        lax.all_gather(neighbour, "feat", axis=1, tiled=True),
    )
    summed = jnp.dot(whole_self, weight[:full_width], preferred_element_type=jnp.float32)
    summed = summed + jnp.dot(whole_pool, weight[full_width:], preferred_element_type=jnp.float32)
    summed = summed + bias.astype(jnp.float32)[None, :]
    return jnp.maximum(summed, 0.0).astype(jnp.bfloat16)


def solution(mesh):
    return jax.shard_map(
        shards,
        mesh=mesh,
        in_specs=(
            P("dom", "feat"),
            P(None, "feat"),
            P("feat"),
            P("dom"),
            P("dom"),
            P("dom"),
            P("dom"),
            P("dom"),
            P("dom", None),
            P("dom"),
            P("dom"),
        ),
        out_specs=P("dom", "feat"),
        check_vma=False,
    )
```

profile of v0, /device:TPU:2, one launch (start us, length us, event | category | flops | bytes accessed | tf_op | source)
XLA Modules:
  0.0 212.0 jit_solution(16495056417987468175)
XLA Ops:
  0.0 0.8 compare_select_fusion.1
  0.8 0.9 copy.34
  1.7 0.1 copy.39
  1.9 0.1 copy.38
  2.0 1.9 gather_fusion.1
  3.9 0.2 bitcast_select_fusion
  4.0 0.8 reshape.165
  4.8 19.2 %all-to-all-start = ((bf16[96,2,128]{2,1,0:T(2,128)(2,1)}), bf16[96,2,128]{2,1,0:T(2,128)(2,1)S(1)}, u32[]{:S(2)}, u32[]{:S(2)}) async-start(bf16[96,2,128]{2,1,0:T(2,128)(2,1)} %reshape.165), calls=%async_computation | async-start | bytes 98304 | tf_op jit(solution)/shard_map/all_to_all | solution.py:36
  24.2 0.7 copy-done.5
  24.9 26.5 %all_gather.9 = bf16[512,256]{0,1:T(8,128)(2,1)S(1)} all-gather(bf16[512,32]{0,1:T(8,128)(2,1)S(1)} %copy-done), channel_id=1, replica_groups=mesh['dom'=96,'feat'=8] {'feat'}, dimensions={1}, use_global_device_ids=true | all-gather | bytes 294912 | tf_op jit(solution)/shard_map/all_gather | solution.py:46
  51.4 0.6 gather_fusion
  52.0 64.1 %all_gather.10 = bf16[1536,32]{1,0:T(8,128)(2,1)S(1)} all-gather(bf16[16,32]{1,0:T(8,128)(2,1)S(1)} %broadcast_select_fusion), channel_id=1, replica_groups=mesh['dom'=96,'feat'=8] {'dom'}, dimensions={0}, use_global_device_ids=true | all-gather | bytes 99328 | tf_op jit(solution)/shard_map/all_gather | solution.py:34
  116.1 7.7 %scatter_custom_fusion.4 = f32[512]{0:T(512)S(1)} fusion(s32[1024]{0:T(1024)} %param.18, f32[1024]{0:T(1024)S(1)} %broadcast.38, f32[]{:T(128)} %constant.54.clone.1), kind=kCustom, calls=%fused_computation.54 | custom fusion | flops 1024 | bytes 2560 | tf_op jit(solution)/shard_map/scatter-add | solution.py:14
  123.9 14.8 %scatter_custom_fusion.3 = f32[512]{0:T(512)S(1)} fusion(s32[2048]{0:T(1024)} %param.15, f32[2048]{0:T(1024)S(1)} %broadcast.37, f32[]{:T(128)} %constant.54.clone.1), kind=kCustom, calls=%fused_computation.56 | custom fusion | flops 2048 | bytes 2560 | tf_op jit(solution)/shard_map/scatter-add | solution.py:14
  138.7 19.2 %scatter_custom_fusion = f32[512,32]{1,0:T(8,128)S(1)} fusion(s32[2048]{0:T(1024)} %param.15, pred[2048]{0:T(1024)(128)(4,1)S(1)} %compare_and_fusion, bf16[]{:T(256)} %constant.58.clone.1, f32[]{:T(128)} %constant.54.clone.1, bf16[512,32]{1,0:T(8,128)(2,1)S(1)} %copy.34, s32[2048]{0:T(1024)S(1)} %fusion.23), kind=kCustom, calls=%fused_computation.15 | custom fusion | flops 196608 | bytes 109568 | tf_op jit(solution)/shard_map/scatter-add | solution.py:8
  157.8 9.9 %scatter_custom_fusion.1 = f32[512,32]{1,0:T(8,128)S(1)} fusion(s32[1024]{0:T(1024)} %param.18, pred[1024]{0:T(1024)(128)(4,1)S(1)} %compare_and_fusion.3, f32[]{:T(128)} %constant.54.clone.1, bf16[]{:T(256)} %constant.58.clone.1, bf16[1536,32]{1,0:T(8,128)(2,1)S(1)} %all_gather.10, s32[1024]{0:T(1024)S(1)} %fusion.24), kind=kCustom, calls=%fused_computation.19 | custom fusion | flops 98304 | bytes 169984 | tf_op jit(solution)/shard_map/scatter-add | solution.py:8
  167.8 0.7 copy-done.6
  168.5 7.6 %scatter_fusion = f32[512]{0:T(512)S(1)} fusion(f32[512]{0:T(512)S(1)} %add.79, s32[1024]{0:T(1024)S(1)} %copy-done.6, f32[1024]{0:T(1024)S(1)} %broadcast.38), kind=kCustom, calls=%fused_computation.10 | custom fusion | flops 1024 | bytes 16384 | tf_op jit(solution)/shard_map/scatter-add | solution.py:14
  176.1 0.1 fusion.21
  176.3 0.1 reshape.166
  176.4 9.9 %scatter_custom_fusion.2 = f32[512,32]{1,0:T(8,128)S(1)} fusion(f32[512,32]{1,0:T(8,128)S(1)} %add.74, s32[1024]{0:T(1024)S(1)} %copy-done.6, pred[1024]{0:T(1024)(128)(4,1)S(1)} %compare_and_fusion.2, bf16[]{:T(256)} %constant.58.clone.1, bf16[768,32]{1,0:T(8,128)(2,1)S(1)} %bitcast.5, s32[1024]{0:T(1024)S(1)} %fusion.25), kind=kCustom, calls=%fused_computation.17 | custom fusion | flops 98304 | bytes 267266 | tf_op jit(solution)/shard_map/scatter-add | solution.py:8
  186.3 0.1 copy.41
  186.4 24.9 %all_gather.11 = bf16[512,256]{0,1:T(8,128)(2,1)S(1)} all-gather(bf16[512,32]{0,1:T(8,128)(2,1)S(1)} %divide_convert_fusion), channel_id=1, replica_groups=mesh['dom'=96,'feat'=8] {'feat'}, dimensions={1}, use_global_device_ids=true | all-gather | bytes 294912 | tf_op jit(solution)/shard_map/all_gather | solution.py:47
  211.3 0.8 fusion.2
  (37 shorter events, 0.3 us)
Async XLA Ops:
  0.0 0.8 copy-start.3
  4.8 19.2 %copy-start.7 = (s32[16]{0:T(128)S(1)}, s32[16]{0:T(128)}, u32[]{:S(2)}) copy-start(s32[16]{0:T(128)} %param.16) | copy-start | bytes 196
  4.8 19.3 %copy-start.4 = (s32[1024]{0:T(1024)S(1)}, s32[1024]{0:T(1024)}, u32[]{:S(2)}) copy-start(s32[1024]{0:T(1024)} %param.17) | copy-start | bytes 12292
  4.8 19.3 %copy-start.1 = (s32[2048]{0:T(1024)S(1)}, s32[2048]{0:T(1024)}, u32[]{:S(2)}) copy-start(s32[2048]{0:T(1024)} %param.14) | copy-start | bytes 24580
  4.8 171.4 %all-to-all-start = ((bf16[96,2,128]{2,1,0:T(2,128)(2,1)}), bf16[96,2,128]{2,1,0:T(2,128)(2,1)S(1)}, u32[]{:S(2)}, u32[]{:S(2)}) async-start(bf16[96,2,128]{2,1,0:T(2,128)(2,1)} %reshape.165), calls=%async_computation | async-start | bytes 98304 | tf_op jit(solution)/shard_map/all_to_all | solution.py:36
  24.1 0.8 copy-start
  24.2 0.7 copy-start.5
  52.0 64.1 %copy-start.8 = (bf16[32]{0:T(256)(128)(2,1)S(1)}, bf16[32]{0:T(256)(128)(2,1)}, u32[]{:S(2)}) copy-start(bf16[32]{0:T(256)(128)(2,1)} %param.13) | copy-start | bytes 196
  167.8 0.7 copy-start.6
  168.5 7.6 %copy-start.2 = (bf16[512,32]{0,1:T(8,128)(2,1)S(1)}, bf16[512,32]{0,1:T(8,128)(2,1)}, u32[]{:S(2)}) copy-start(bf16[512,32]{0,1:T(8,128)(2,1)} %param.12) | copy-start | bytes 98308
where the time goes:
time: 213 us; the launch traced here: 212 us
  blocking collectives  115 us (54%)
  other arithmetic  70.2 us (33%)
  starting transfers between devices  19.2 us (9%)
  local copies, waits for them, and re-layouts  6 us (3%)
    all_gather x1, blocking collectives, shards(): hub_table = lax.all_gather(hub_local, 'dom', axis=0, tiled=True)  64.1 us
    scatter-add x3, other arithmetic, pool_rows(): jax.ops.segment_sum(jnp.take(table, source, axis=0).astype(jnp.float32),...  38.9 us
    scatter-add x3, other arithmetic, count_edges(): jax.ops.segment_sum(jnp.ones(target.shape, jnp.float32), target, num_segm...  30.2 us
    all_gather x1, blocking collectives, shards(): lax.all_gather(features, 'feat', axis=1, tiled=True)  26.5 us
    all_gather x1, blocking collectives, shards(): lax.all_gather(neighbour, 'feat', axis=1, tiled=True)  24.9 us
    all_to_all x1, starting transfers between devices, shards(): lax.all_to_all(outgoing, 'dom', split_axis=0, concat_axis=0, tiled=True)  19.2 us
  transfers between devices with their start and end apart: 1, of which 0 were waited for; matrix products, arithmetic and copies ran while one was open for 28% of the time, Pallas kernels for 0%

commit v1 on v0

v1 whole, which is shorter than its diff:
```python
import jax
import jax.numpy as jnp
from jax import lax
from jax.experimental import pallas as pl
from jax.experimental.pallas import tpu as pltpu
from jax.sharding import PartitionSpec as P

MESH = pl.DeviceIdType.MESH
BF = jnp.bfloat16
F32 = jnp.float32
NX, NZ, NY = 4, 12, 8
NQ = NX * NZ
NODES = 512
W = 32
ROWS = NQ * 8
HALF = 4 * ROWS
EDGES = 2048


def dist(step, size):
    return min(step, size - step)


OFFSETS = sorted(
    [(dx, dz) for dx in range(NX) for dz in range(NZ) if (dx, dz) != (0, 0)],
    key=lambda o: -(dist(o[0], NX) + dist(o[1], NZ)),
)
Y_ORDER = (4, 3, 5, 2, 6, 1, 7)


def nt(a, b):
    return lax.dot_general(a, b, (((1,), (1,)), ((), ())), preferred_element_type=F32)


def nn(a, b):
    return jnp.dot(a, b, preferred_element_type=F32)


def one_hot(row, size):
    at = lax.broadcasted_iota(jnp.int32, (size, row.shape[1]), 0)
    return jnp.where(at == row, 1.0, 0.0).astype(BF)


def kernel(
    x_hbm, w_hbm, b_hbm, ls_hbm, ld_hbm, hr_hbm, hs_hbm, hd_hbm, sr_hbm, bs_hbm, bd_hbm,
    o_ref,
    w_v, b_v, ls_v, ld_v, hr_v, es_v, ed_v, sr_v, xg, ot, ld1, ls1, ed1, es1, al, ar, pick,
    sendb, recv, in_sem, y_send, y_recv, d_send, d_recv, c_send, c_recv,
):
    dom, f = lax.axis_index("dom"), lax.axis_index("feat")
    core = dom % 2
    q = dom // 2
    z, x = q % NZ, q // NZ

    def chip(dx, dz):
        return lax.rem(x + dx, NX) * NZ + lax.rem(z + dz, NZ)

    sibling = q * 2 + (1 - core)
    barrier = pltpu.get_barrier_semaphore()
    for dx, dz in OFFSETS:
        pl.semaphore_signal(
            barrier, inc=1, device_id={"dom": chip(dx, dz) * 2 + core}, device_id_type=MESH
        )
    for i in Y_ORDER:
        pl.semaphore_signal(
            barrier, inc=1, device_id={"feat": lax.rem(f + i, NY)}, device_id_type=MESH
        )
    pl.semaphore_signal(barrier, inc=1, device_id={"dom": sibling}, device_id_type=MESH)

    loads = []
    for n, (src, dst) in enumerate((
        (x_hbm, xg.at[f]), (sr_hbm, sr_v), (hr_hbm, hr_v), (w_hbm, w_v), (b_hbm, b_v),
        (ls_hbm, ls_v), (ld_hbm, ld_v),
        (hs_hbm, es_v.at[pl.ds(0, 8)]), (bs_hbm, es_v.at[pl.ds(8, 8)]),
        (hd_hbm, ed_v.at[pl.ds(0, 8)]), (bd_hbm, ed_v.at[pl.ds(8, 8)]),
    )):
        copy = pltpu.make_async_copy(src, dst, in_sem.at[n])
        copy.start()
        loads.append(copy)
    for copy in loads:
        copy.wait()

    def send_lists():
        lane = lax.broadcasted_iota(jnp.int32, (16, 512), 1)
        hub = lax.broadcasted_iota(jnp.int32, (16, 512), 0)
        spread = jnp.where(
            (lane // 128 == hub % 4) & (lane % 128 == 96 + hub // 4), 1.0, 0.0
        ).astype(BF)
        hub_lanes = nn(one_hot(hr_v[...], NODES), spread)
        for c in range(8):
            part = one_hot(sr_v[c : c + 1, :], NODES)
            part = jnp.concatenate([part, jnp.zeros((NODES, 32), BF)], axis=1)
            j, si = c % 4, c // 4
            if si == 0:
                part = part + hub_lanes[:, j * 128 : j * 128 + 128].astype(BF)
            ot[:, j * 256 + si * 128 : j * 256 + si * 128 + 128] = part
        row = lax.broadcasted_iota(jnp.int32, (ROWS, 256), 0)
        col = lax.broadcasted_iota(jnp.int32, (ROWS, 256), 1)
        t = row % 8
        want = jnp.where(t < 4, (t % 2) * 128 + (row // 8) * 2 + t // 2, 92 + t)
        pick[...] = jnp.where(col == want, 1.0, 0.0).astype(BF)

    def hot_rows(ref, at, out, size):
        @pl.loop(0, EDGES // 128)
        def _(i):
            lanes = pl.ds(pl.multiple_of(i * 128, 128), 128)
            out[0:size, lanes] = one_hot(ref[pl.ds(i, 1), :] - at, size)

    send_lists()
    pl.semaphore_wait(barrier, len(OFFSETS) + NY)

    sends = []
    for i in Y_ORDER:
        copy = pltpu.make_async_remote_copy(
            src_ref=xg.at[f], dst_ref=xg.at[f], send_sem=y_send, recv_sem=y_recv,
            device_id={"feat": lax.rem(f + i, NY)}, device_id_type=MESH,
        )
        copy.start()

    ls1[NODES : NODES + 16, :] = jnp.ones((16, EDGES), BF)
    es1[ROWS : ROWS + 16, :] = jnp.ones((16, EDGES), BF)
    hot_rows(ls_v, 0, ls1, NODES)
    hot_rows(ld_v, 0, ld1, NODES)
    hot_rows(ed_v, 0, ed1, NODES)
    counts = nt(ls1[...], ld1[...])
    al[...] = counts[:NODES].astype(BF)
    degree = counts[NODES : NODES + 1]

    h = es_v[0:8, :]
    s = h // 16
    es_v[0:8, :] = (s % 2) * HALF + (h % 4) * ROWS + (s // 2) * 8 + 4 + (h // 4) % 4
    b = es_v[8:16, :]
    s = b // 8
    es_v[8:16, :] = (s % 2) * HALF + (b % 4) * ROWS + (s // 2) * 8 + 2 * core + (b // 4) % 2

    def count_block(k):
        hot_rows(es_v, k * ROWS, es1, ROWS)
        got = nt(es1[...], ed1[...])
        ar[pl.ds(pl.multiple_of(k * ROWS, 16), ROWS), :] = got[:ROWS].astype(BF)
        return got[ROWS : ROWS + 1]

    degree = degree + count_block(0)

    @pl.loop(1, 4)
    def _(k):
        count_block(k)

    all_y = pltpu.make_async_copy(xg.at[pl.ds(0, 7)], xg.at[pl.ds(0, 7)], y_recv)
    all_y.wait()

    both = jnp.concatenate([w_v[:, 256:512], w_v[:, 0:256]], axis=0)
    yz = nn(both, xg[...].reshape(NY * W, NODES))
    high = yz[0:W].astype(BF)
    low = (yz[0:W] - high.astype(F32)).astype(BF)
    lists = jnp.concatenate(
        [nn(high, ot[:, j * 256 : j * 256 + 256]) for j in range(4)], axis=0
    ).astype(BF)
    sendb[...] = nt(pick[...], lists).reshape(NQ, 8, 128).astype(BF)

    for dx, dz in OFFSETS:
        to = chip(dx, dz)
        copy = pltpu.make_async_remote_copy(
            src_ref=sendb.at[to], dst_ref=recv.at[core, q], send_sem=d_send, recv_sem=d_recv,
            device_id={"dom": to * 2 + core}, device_id_type=MESH,
        )
        copy.start()
    recv[core, q] = sendb[q]

    @pl.loop(4, 8)
    def _(k):
        count_block(k)

    near = nn(jnp.concatenate([high, low], axis=0), al[...])
    pooled = near[0:W] + near[W : 2 * W]
    diag = lax.broadcasted_iota(jnp.int32, (W, W), 0) == lax.broadcasted_iota(jnp.int32, (W, W), 1)
    bias = jnp.sum(jnp.where(diag, b_v[...].astype(F32), 0.0), axis=1, keepdims=True)
    eye = jnp.where(
        lax.broadcasted_iota(jnp.int32, (128, 128), 0)
        == lax.broadcasted_iota(jnp.int32, (128, 128), 1), 1.0, 0.0,
    ).astype(BF)

    def add_half(side):
        rows = recv[side].reshape(ROWS, 128)
        turned = nt(eye, rows).astype(BF)
        wide = jnp.concatenate([turned[j * W : j * W + W] for j in range(4)], axis=1)
        return nn(wide, ar[pl.ds(pl.multiple_of(side * HALF, 16), HALF), :])

    all_d = pltpu.make_async_copy(recv.at[0, pl.ds(0, NQ - 1)], recv.at[0, pl.ds(0, NQ - 1)], d_recv)
    all_d.wait()
    swap = pltpu.make_async_remote_copy(
        src_ref=recv.at[core], dst_ref=recv.at[core], send_sem=c_send, recv_sem=c_recv,
        device_id={"dom": sibling}, device_id_type=MESH,
    )
    swap.start()
    pooled = pooled + add_half(core)
    swap.wait_recv()
    pooled = pooled + add_half(1 - core)

    out = yz[W : 2 * W] + bias + pooled / jnp.maximum(degree, 1.0)
    o_ref[...] = jnp.maximum(out, 0.0).astype(BF)
    pltpu.make_async_copy(xg.at[pl.ds(0, 7)], xg.at[pl.ds(0, 7)], y_send).wait()
    pltpu.make_async_copy(
        recv.at[0, pl.ds(0, NQ - 1)], recv.at[0, pl.ds(0, NQ - 1)], d_send
    ).wait()
    swap.wait_send()


def shards(
    features, weight, bias, local_src, local_dst, hub_rows, hub_src, hub_dst, send_rows,
    bnd_src, bnd_dst,
):
    V = pltpu.VMEM
    I32 = jnp.int32
    DMA = pltpu.SemaphoreType.DMA
    out = pl.pallas_call(
        kernel,
        out_shape=jax.ShapeDtypeStruct((W, NODES), BF),
        in_specs=[pl.BlockSpec(memory_space=pl.ANY)] * 11,
        out_specs=pl.BlockSpec(memory_space=pltpu.VMEM),
        scratch_shapes=[
            V((W, NODES), BF), V((1, W), BF), V((16, 128), I32), V((16, 128), I32),
            V((1, 16), I32), V((16, 128), I32), V((16, 128), I32), V((8, 96), I32),
            V((NY, W, NODES), BF), V((NODES, 1024), BF),
            V((NODES, EDGES), BF), V((NODES + 16, EDGES), BF),
            V((NODES, EDGES), BF), V((ROWS + 16, EDGES), BF),
            V((NODES, NODES), BF), V((2 * HALF, NODES), BF), V((ROWS, 256), BF),
            V((NQ, 8, 128), BF), V((2, NQ, 8, 128), BF),
            DMA((11,)), DMA(()), DMA(()), DMA(()), DMA(()), DMA(()), DMA(()),
        ],
        compiler_params=pltpu.CompilerParams(
            collective_id=0, has_side_effects=True, vmem_limit_bytes=56 * 1024 * 1024
        ),
    )(
        features.T, weight.T, bias.reshape(1, W),
        local_src.reshape(16, 128), local_dst.reshape(16, 128), hub_rows.reshape(1, 16),
        hub_src.reshape(8, 128), hub_dst.reshape(8, 128), send_rows.T,
        bnd_src.reshape(8, 128), bnd_dst.reshape(8, 128),
    )
    return out.T


def solution(mesh):
    return jax.shard_map(
        shards,
        mesh=mesh,
        in_specs=(
            P("dom", "feat"), P(None, "feat"), P("feat"), P("dom"), P("dom"), P("dom"),
            P("dom"), P("dom"), P("dom", None), P("dom"), P("dom"),
        ),
        out_specs=P("dom", "feat"),
        check_vma=False,
    )
```

time: 213 us -> 41 us (0.19)
  the two profiles are of different devices: /device:TPU:2 before, /device:TPU:1 now
where the time goes in v1:
time: 41 us; the launch traced here: 40.7 us
  Pallas kernels  39.3 us (96%)
  local copies, waits for them, and re-layouts  1.38 us (3%)
    pallas_call x1, Pallas kernels, shards(): pl.pallas_call(kernel, out_shape=jax.ShapeDtypeStruct((W, NODES), BF), in...  39.3 us
    unnamed x1, local copies, waits for them, and re-layouts  1.38 us

profile of v1, /device:TPU:1, one launch (start us, length us, event | category | flops | bytes accessed | tf_op | source)
XLA Modules:
  0.0 40.7 jit_solution(13137652384037582657)
XLA Ops:
  0.0 39.3 %shard_map.109 = bf16[32,512]{1,0:T(8,128)(2,1)} custom-call(bf16[32,512]{1,0:T(8,128)(2,1)} %bitcast.13, bf16[32,512]{1,0:T(8,128)(2,1)} %bitcast.14, bf16[1,32]{1,0:T(2,128)(2,1)} %bitcast.22, s32[16,128]{1,0:T(8,128)} %bitcast.15, s32[16,128]{1,0:T(8,128)} %bitcast.16, s32[1,16]{1,0:T(1,128)} %bitcast.23, s32[8,128]{1,0:T(8,128)} %bitcast.17, ...), custom_call_target="tpu_custom_call" | custom-call | tf_op jit(solution)/shard_map/pallas_call | solution.py:215
  39.3 1.4 %copy.13 = bf16[512,32]{0,1:T(8,128)(2,1)} copy(bf16[512,32]{0,1:T(8,128)(2,1)} %bitcast.12) | data formatting | bytes 65536

commit v2 on v1

v2 whole, which is shorter than its diff:
```python
import jax
import jax.numpy as jnp
from jax import lax
from jax.experimental import pallas as pl
from jax.experimental.pallas import tpu as pltpu
from jax.sharding import PartitionSpec as P

MESH = pl.DeviceIdType.MESH
BF = jnp.bfloat16
F32 = jnp.float32
NX, NZ, NY = 4, 12, 8
NG = NX * 2
NODES = 512
W = 32
EDGES = 2048
SPAN = 4
PART = SPAN * NG * 8
PARTS = NZ // SPAN
Y_ORDER = (4, 3, 5, 2, 6, 1, 7)


def nt(a, b):
    return lax.dot_general(a, b, (((1,), (1,)), ((), ())), preferred_element_type=F32)


def nn(a, b):
    return jnp.dot(a, b, preferred_element_type=F32)


def one_hot(row, size):
    at = lax.broadcasted_iota(jnp.int32, (size, row.shape[1]), 0)
    return jnp.where(at == row, 1.0, 0.0).astype(BF)


def kernel(
    x_hbm, w_hbm, b_hbm, ls_hbm, ld_hbm, hr_hbm, hs_hbm, hd_hbm, sr_hbm, bs_hbm, bd_hbm,
    o_ref,
    w_v, b_v, ls_v, ld_v, hr_v, es_v, ed_v, sr_v, xg, ng, ot, ld1, ls1, ed1, es1, al, ar, pick,
    sendb, recv, in_sem, ready, x_send, x_recv, n_send, n_recv, d_send, d_recv,
):
    dom, f = lax.axis_index("dom"), lax.axis_index("feat")
    core = dom % 2
    z, x = (dom // 2) % NZ, dom // (2 * NZ)
    me = 2 * x + core

    def device(zz, n):
        return {"dom": ((n // 2) * NZ + zz) * 2 + n % 2}

    rank = jnp.where(f <= NY // 2, jnp.maximum(2 * f - 1, 0), 2 * (NY - f))

    def at_rank(r):
        return {"feat": jnp.where(r % 2 == 1, (r + 1) // 2, lax.rem(NY - r // 2, NY))}

    barrier = pltpu.get_barrier_semaphore()

    def greet(device_id):
        pl.semaphore_signal(barrier, inc=1, device_id=device_id, device_id_type=MESH)

    loads = []
    for n, (src, dst) in enumerate((
        (sr_hbm, sr_v), (hr_hbm, hr_v), (x_hbm, xg.at[f]), (w_hbm, w_v), (b_hbm, b_v),
        (ls_hbm, ls_v), (ld_hbm, ld_v),
        (hs_hbm, es_v.at[pl.ds(0, 8)]), (bs_hbm, es_v.at[pl.ds(8, 8)]),
        (hd_hbm, ed_v.at[pl.ds(0, 8)]), (bd_hbm, ed_v.at[pl.ds(8, 8)]),
    )):
        copy = pltpu.make_async_copy(src, dst, in_sem.at[n])
        copy.start()
        loads.append(copy)

    for n in range(1, NG):
        greet(device(z, lax.rem(me + n, NG)))

    @pl.loop(rank + 1, NY)
    def _(r):
        greet(at_rank(r))

    @pl.loop(z + 1, NZ)
    def _(zz):
        for n in range(NG):
            greet(device(zz, n))

    row = lax.broadcasted_iota(jnp.int32, (NZ * NX * 8, 256), 0)
    col = lax.broadcasted_iota(jnp.int32, (NZ * NX * 8, 256), 1)
    t, to = row % 8, row // 8
    to = (to % NX) * NZ + to // NX
    want = jnp.where(t < 4, (t % 2) * 128 + to * 2 + t // 2, 92 + t)
    pick[...] = jnp.where(col == want, 1.0, 0.0).astype(BF)

    for copy in loads:
        copy.wait()

    lane = lax.broadcasted_iota(jnp.int32, (16, 512), 1)
    hub = lax.broadcasted_iota(jnp.int32, (16, 512), 0)
    spread = jnp.where(
        (lane // 128 == hub % 4) & (lane % 128 == 96 + hub // 4), 1.0, 0.0
    ).astype(BF)
    hub_lanes = nn(one_hot(hr_v[...], NODES), spread)
    for c in range(8):
        part = one_hot(sr_v[c : c + 1, :], NODES)
        part = jnp.concatenate([part, jnp.zeros((NODES, 32), BF)], axis=1)
        j, si = c % 4, c // 4
        if si == 0:
            part = part + hub_lanes[:, j * 128 : j * 128 + 128].astype(BF)
        ot[:, j * 256 + si * 128 : j * 256 + si * 128 + 128] = part
    own = xg[f]
    lists = jnp.concatenate(
        [nn(own, ot[:, j * 256 : j * 256 + 256]) for j in range(4)], axis=0
    ).astype(BF)
    sendb[...] = nt(pick[...], lists).reshape(NZ * NX, 8, 128).astype(BF)

    def send(zz, n, index):
        pltpu.make_async_remote_copy(
            src_ref=sendb.at[zz * NX + n // 2], dst_ref=recv.at[z, me],
            send_sem=d_send.at[index], recv_sem=d_recv.at[index if index is NZ else z],
            device_id=device(zz, n), device_id_type=MESH,
        ).start()

    def send_plane(zz):
        for n in range(NG):
            send(zz, n, zz)

    def plane_of(sem, count):
        region = recv.at[0, pl.ds(0, count)]
        return pltpu.make_async_copy(region, region, sem)

    pl.semaphore_wait(barrier, NG * z + NG - 1 + rank)

    @pl.loop(0, z)
    def _(zz):
        send_plane(zz)

    for n in range(1, NG):
        send(z, lax.rem(me + n, NG), NZ)

    @pl.loop(0, rank)
    def _(r):
        pl.semaphore_signal(ready, inc=1, device_id=at_rank(r), device_id_type=MESH)

    recv[z, me] = sendb[z * NX + x]

    def hot_rows(ref, at, out, size):
        @pl.loop(0, EDGES // 128)
        def _(i):
            lanes = pl.ds(pl.multiple_of(i * 128, 128), 128)
            out[0:size, lanes] = one_hot(ref[pl.ds(i, 1), :] - at, size)

    ls1[NODES : NODES + 16, :] = jnp.ones((16, EDGES), BF)
    es1[PART : PART + 16, :] = jnp.ones((16, EDGES), BF)
    hot_rows(ls_v, 0, ls1, NODES)
    hot_rows(ld_v, 0, ld1, NODES)
    counts = nt(ls1[...], ld1[...])
    al[...] = counts[:NODES].astype(BF)
    degree = counts[NODES : NODES + 1]
    pooled = nn(own, al[...])

    def to_peers(block, send_sem, recv_sem):
        for i in Y_ORDER:
            pltpu.make_async_remote_copy(
                src_ref=block.at[f], dst_ref=block.at[f], send_sem=send_sem, recv_sem=recv_sem,
                device_id={"feat": lax.rem(f + i, NY)}, device_id_type=MESH,
            ).start()

    def peers_of(block, sem):
        region = block.at[pl.ds(0, NY - 1)]
        return pltpu.make_async_copy(region, region, sem)

    @pl.when(rank < NY - 1)
    def _():
        pl.semaphore_wait(ready, NY - 1 - rank)

    to_peers(xg, x_send, x_recv)

    def slots(s, j, t):
        half = s // 2
        xx = half // NZ
        zz = half - xx * NZ
        line = zz * (NG * 8) + (2 * xx + s % 2) * 8 + t
        return (line // PART) * (4 * PART) + j * PART + line % PART

    h = es_v[0:8, :]
    es_v[0:8, :] = slots(h // 16, h % 4, 4 + (h // 4) % 4)
    b = es_v[8:16, :]
    es_v[8:16, :] = slots(b // 8, b % 4, 2 * core + (b // 4) % 2)

    def count_block(k):
        hot_rows(es_v, k * PART, es1, PART)
        got = nt(es1[...], ed1[...])
        ar[pl.ds(pl.multiple_of(k * PART, 16), PART), :] = got[:PART].astype(BF)
        return got[PART : PART + 1]

    hot_rows(ed_v, 0, ed1, NODES)
    degree = degree + count_block(0)

    @pl.loop(1, 4 * PARTS)
    def _(k):
        count_block(k)

    scale = 1.0 / jnp.maximum(degree, 1.0)
    diag = lax.broadcasted_iota(jnp.int32, (W, W), 0) == lax.broadcasted_iota(jnp.int32, (W, W), 1)
    bias = jnp.sum(jnp.where(diag, b_v[...].astype(F32), 0.0), axis=1, keepdims=True)
    peers_of(xg, x_recv).wait()
    own_term = nn(w_v[:, 0:256], xg[...].reshape(NY * W, NODES)) + bias
    eye = jnp.where(
        lax.broadcasted_iota(jnp.int32, (128, 128), 0)
        == lax.broadcasted_iota(jnp.int32, (128, 128), 1), 1.0, 0.0,
    ).astype(BF)

    for part in range(PARTS):
        @pl.loop(part * SPAN, part * SPAN + SPAN)
        def _(zz):
            @pl.when(zz == z)
            def _():
                plane_of(d_recv.at[NZ], NG - 1).wait()

            @pl.when(zz != z)
            def _():
                plane_of(d_recv.at[zz], NG).wait()

            @pl.when((zz > z) & (zz < NZ - 1))
            def _():
                send_plane(zz)

        rows = recv[part * SPAN : part * SPAN + SPAN].reshape(PART, 128)
        turned = nt(eye, rows).astype(BF)
        wide = jnp.concatenate([turned[j * W : j * W + W] for j in range(4)], axis=1)
        pooled = pooled + nn(wide, ar[part * 4 * PART : (part + 1) * 4 * PART, :])

    ng[f] = (pooled * scale).astype(BF)
    to_peers(ng, n_send, n_recv)

    @pl.when(z < NZ - 1)
    def _():
        send_plane(NZ - 1)

    peers_of(ng, n_recv).wait()
    out = own_term + nn(w_v[:, 256:512], ng[...].reshape(NY * W, NODES))
    o_ref[...] = jnp.maximum(out, 0.0).astype(BF)

    peers_of(xg, x_send).wait()
    peers_of(ng, n_send).wait()
    plane_of(d_send.at[NZ], NG - 1).wait()

    @pl.loop(0, NZ)
    def _(zz):
        @pl.when(zz != z)
        def _():
            plane_of(d_send.at[zz], NG).wait()


def shards(
    features, weight, bias, local_src, local_dst, hub_rows, hub_src, hub_dst, send_rows,
    bnd_src, bnd_dst,
):
    V = pltpu.VMEM
    I32 = jnp.int32
    DMA = pltpu.SemaphoreType.DMA
    out = pl.pallas_call(
        kernel,
        out_shape=jax.ShapeDtypeStruct((W, NODES), BF),
        in_specs=[pl.BlockSpec(memory_space=pl.ANY)] * 11,
        out_specs=pl.BlockSpec(memory_space=pltpu.VMEM),
        scratch_shapes=[
            V((W, NODES), BF), V((1, W), BF), V((16, 128), I32), V((16, 128), I32),
            V((1, 16), I32), V((16, 128), I32), V((16, 128), I32), V((8, 96), I32),
            V((NY, W, NODES), BF), V((NY, W, NODES), BF), V((NODES, 1024), BF),
            V((NODES, EDGES), BF), V((NODES + 16, EDGES), BF),
            V((NODES, EDGES), BF), V((PART + 16, EDGES), BF),
            V((NODES, NODES), BF), V((4 * PART * PARTS, NODES), BF), V((NZ * NX * 8, 256), BF),
            V((NZ * NX, 8, 128), BF), V((NZ, NG, 8, 128), BF),
            DMA((11,)), pltpu.SemaphoreType.REGULAR, DMA(()), DMA(()), DMA(()), DMA(()),
            DMA((NZ + 1,)), DMA((NZ + 1,)),
        ],
        compiler_params=pltpu.CompilerParams(
            collective_id=0, has_side_effects=True, vmem_limit_bytes=56 * 1024 * 1024
        ),
    )(
        features.T, weight.T, bias.reshape(1, W),
        local_src.reshape(16, 128), local_dst.reshape(16, 128), hub_rows.reshape(1, 16),
        hub_src.reshape(8, 128), hub_dst.reshape(8, 128), send_rows.T,
        bnd_src.reshape(8, 128), bnd_dst.reshape(8, 128),
    )
    return out.T


def solution(mesh):
    return jax.shard_map(
        shards,
        mesh=mesh,
        in_specs=(
            P("dom", "feat"), P(None, "feat"), P("feat"), P("dom"), P("dom"), P("dom"),
            P("dom"), P("dom"), P("dom", None), P("dom"), P("dom"),
        ),
        out_specs=P("dom", "feat"),
        check_vma=False,
    )
```

time: 41 us -> 75.7 us (1.85)
  the two profiles are of different devices: /device:TPU:1 before, /device:TPU:705 now
where the time goes in v2:
time: 75.7 us; the launch traced here: 75.5 us
  Pallas kernels  74.1 us (98%)
  local copies, waits for them, and re-layouts  1.38 us (2%)
    pallas_call x1, Pallas kernels, shards(): pl.pallas_call(kernel, out_shape=jax.ShapeDtypeStruct((W, NODES), BF), in...  74.1 us

profile of v2, /device:TPU:705, one launch (start us, length us, event | category | flops | bytes accessed | tf_op | source)
XLA Modules:
  0.0 75.5 jit_solution(11786088154104139231)
XLA Ops:
  0.0 74.1 %shard_map.109 = bf16[32,512]{1,0:T(8,128)(2,1)} custom-call(bf16[32,512]{1,0:T(8,128)(2,1)} %bitcast.13, bf16[32,512]{1,0:T(8,128)(2,1)} %bitcast.14, bf16[1,32]{1,0:T(2,128)(2,1)} %bitcast.22, s32[16,128]{1,0:T(8,128)} %bitcast.15, s32[16,128]{1,0:T(8,128)} %bitcast.16, s32[1,16]{1,0:T(1,128)} %bitcast.23, s32[8,128]{1,0:T(8,128)} %bitcast.17, ...), custom_call_target="tpu_custom_call" | custom-call | tf_op jit(solution)/shard_map/pallas_call | solution.py:257
  74.1 1.4 %copy.13 = bf16[512,32]{0,1:T(8,128)(2,1)} copy(bf16[512,32]{0,1:T(8,128)(2,1)} %bitcast.12) | data formatting | bytes 65536

commit v3 on v2

--- a/solution.py
+++ b/solution.py
@@ -14,8 +14,13 @@
 W = 32
 EDGES = 2048
 SPAN = 4
-PART = SPAN * NG * 8
+LINES = SPAN * NG * 8
 PARTS = NZ // SPAN
+HUB_PART = SPAN * NG * 4
+BND_PART = SPAN * NG * 2
+PART = 4 * (HUB_PART + BND_PART)
+EARLY = 3
+LATE = NZ // 2
 Y_ORDER = (4, 3, 5, 2, 6, 1, 7)
 
 
@@ -36,7 +41,7 @@
     x_hbm, w_hbm, b_hbm, ls_hbm, ld_hbm, hr_hbm, hs_hbm, hd_hbm, sr_hbm, bs_hbm, bd_hbm,
     o_ref,
     w_v, b_v, ls_v, ld_v, hr_v, es_v, ed_v, sr_v, xg, ng, ot, ld1, ls1, ed1, es1, al, ar, pick,
-    sendb, recv, in_sem, ready, x_send, x_recv, n_send, n_recv, d_send, d_recv,
+    sel, acc, sendb, recv, in_sem, ready, x_send, x_recv, n_send, n_recv, d_send, d_recv,
 ):
     dom, f = lax.axis_index("dom"), lax.axis_index("feat")
     core = dom % 2
@@ -74,10 +79,13 @@
     def _(r):
         greet(at_rank(r))
 
-    @pl.loop(z + 1, NZ)
-    def _(zz):
-        for n in range(NG):
-            greet(device(zz, n))
+    def greet_up():
+        @pl.loop(z + 1, NZ)
+        def _(zz):
+            for n in range(NG):
+                greet(device(zz, n))
+
+    pl.when(z >= EARLY)(greet_up)
 
     row = lax.broadcasted_iota(jnp.int32, (NZ * NX * 8, 256), 0)
     col = lax.broadcasted_iota(jnp.int32, (NZ * NX * 8, 256), 1)
@@ -136,16 +144,18 @@
     def _(r):
         pl.semaphore_signal(ready, inc=1, device_id=at_rank(r), device_id_type=MESH)
 
+    pl.when(z < EARLY)(greet_up)
+
     recv[z, me] = sendb[z * NX + x]
 
-    def hot_rows(ref, at, out, size):
-        @pl.loop(0, EDGES // 128)
+    def hot_rows(ref, at, out, size, first=0):
+        @pl.loop(0, out.shape[1] // 128)
         def _(i):
             lanes = pl.ds(pl.multiple_of(i * 128, 128), 128)
-            out[0:size, lanes] = one_hot(ref[pl.ds(i, 1), :] - at, size)
+            out[0:size, lanes] = one_hot(ref[pl.ds(first + i, 1), :] - at, size)
 
     ls1[NODES : NODES + 16, :] = jnp.ones((16, EDGES), BF)
-    es1[PART : PART + 16, :] = jnp.ones((16, EDGES), BF)
+    es1[4 * HUB_PART : 4 * HUB_PART + 16, :] = jnp.ones((16, EDGES // 2), BF)
     hot_rows(ls_v, 0, ls1, NODES)
     hot_rows(ld_v, 0, ld1, NODES)
     counts = nt(ls1[...], ld1[...])
@@ -170,68 +180,113 @@
 
     to_peers(xg, x_send, x_recv)
 
-    def slots(s, j, t):
+    def slots(s, j, position, width):
         half = s // 2
         xx = half // NZ
         zz = half - xx * NZ
-        line = zz * (NG * 8) + (2 * xx + s % 2) * 8 + t
-        return (line // PART) * (4 * PART) + j * PART + line % PART
+        size = SPAN * NG * width
+        line = (zz * NG + 2 * xx + s % 2) * width + position
+        return (line // size) * (4 * size) + j * size + line % size
 
     h = es_v[0:8, :]
-    es_v[0:8, :] = slots(h // 16, h % 4, 4 + (h // 4) % 4)
+    es_v[0:8, :] = slots(h // 16, h % 4, (h // 4) % 4, 4)
     b = es_v[8:16, :]
-    es_v[8:16, :] = slots(b // 8, b % 4, 2 * core + (b // 4) % 2)
-
-    def count_block(k):
-        hot_rows(es_v, k * PART, es1, PART)
-        got = nt(es1[...], ed1[...])
-        ar[pl.ds(pl.multiple_of(k * PART, 16), PART), :] = got[:PART].astype(BF)
-        return got[PART : PART + 1]
+    es_v[8:16, :] = slots(b // 8, b % 4, (b // 4) % 2, 2)
 
     hot_rows(ed_v, 0, ed1, NODES)
-    degree = degree + count_block(0)
-
-    @pl.loop(1, 4 * PARTS)
-    def _(k):
-        count_block(k)
+    hot_rows(es_v, 0, es1, 4 * HUB_PART)
+    got = nt(es1[...], ed1[...])
+    ar[0 : 4 * HUB_PART, :] = got[: 4 * HUB_PART].astype(BF)
+    degree = degree + got[4 * HUB_PART : 4 * HUB_PART + 1]
+
+    for k in range(1, PARTS):
+        hot_rows(es_v, k * (4 * HUB_PART), es1, 4 * HUB_PART)
+        got = nt(es1[0 : 4 * HUB_PART, :], ed1[...])
+        ar[pl.ds(k * PART, 4 * HUB_PART), :] = got.astype(BF)
+
+    half = 4 * BND_PART
+    hot_rows(ed_v, 0, ed1, NODES, 8)
+    degree = degree + nt(es1[4 * HUB_PART : 4 * HUB_PART + 16, :], ed1[...])[0:1]
+
+    for k in range(PARTS):
+        hot_rows(es_v, k * half, es1, half, 8)
+        got = nt(es1[0:half, :], ed1[...])
+        ar[pl.ds(k * PART + 4 * HUB_PART, half), :] = got.astype(BF)
 
     scale = 1.0 / jnp.maximum(degree, 1.0)
+    acc[...] = pooled
     diag = lax.broadcasted_iota(jnp.int32, (W, W), 0) == lax.broadcasted_iota(jnp.int32, (W, W), 1)
     bias = jnp.sum(jnp.where(diag, b_v[...].astype(F32), 0.0), axis=1, keepdims=True)
-    peers_of(xg, x_recv).wait()
-    own_term = nn(w_v[:, 0:256], xg[...].reshape(NY * W, NODES)) + bias
     eye = jnp.where(
         lax.broadcasted_iota(jnp.int32, (128, 128), 0)
         == lax.broadcasted_iota(jnp.int32, (128, 128), 1), 1.0, 0.0,
     ).astype(BF)
-
-    for part in range(PARTS):
-        @pl.loop(part * SPAN, part * SPAN + SPAN)
-        def _(zz):
-            @pl.when(zz == z)
-            def _():
-                plane_of(d_recv.at[NZ], NG - 1).wait()
-
-            @pl.when(zz != z)
-            def _():
-                plane_of(d_recv.at[zz], NG).wait()
-
-            @pl.when((zz > z) & (zz < NZ - 1))
-            def _():
-                send_plane(zz)
-
-        rows = recv[part * SPAN : part * SPAN + SPAN].reshape(PART, 128)
-        turned = nt(eye, rows).astype(BF)
-        wide = jnp.concatenate([turned[j * W : j * W + W] for j in range(4)], axis=1)
-        pooled = pooled + nn(wide, ar[part * 4 * PART : (part + 1) * 4 * PART, :])
-
-    ng[f] = (pooled * scale).astype(BF)
+    line = lax.broadcasted_iota(jnp.int32, (LINES, 256), 0)
+    at = lax.broadcasted_iota(jnp.int32, (LINES, 256), 1)
+    low = at - HUB_PART
+    want = jnp.where(low < 0, (at // 4) * 8 + 4 + at % 4, (low // 2) * 8 + 2 * core + low % 2)
+    sel[...] = jnp.where((line == want) & (low < BND_PART), 1.0, 0.0).astype(BF)
+
+    def pool(part):
+        rows = recv[part * SPAN : part * SPAN + SPAN].reshape(LINES, 128)
+        turned = nn(nt(eye, rows).astype(BF), sel[...]).astype(BF)
+        wide = jnp.concatenate(
+            [turned[j * W : j * W + W, 0:HUB_PART] for j in range(4)]
+            + [turned[j * W : j * W + W, HUB_PART : HUB_PART + BND_PART] for j in range(4)],
+            axis=1,
+        )
+        acc[...] += nn(wide, ar[part * PART : (part + 1) * PART, :])
+
+    def arrive(zz):
+        plane_of(d_recv.at[zz], NG).wait()
+
+    def arrive_and_answer(zz):
+        arrive(zz)
+        send_plane(zz)
+
+    @pl.when(z == 0)
+    def _():
+        plane_of(d_recv.at[NZ], NG - 1).wait()
+        pl.loop(1, SPAN)(arrive_and_answer)
+
+    @pl.when(z > 0)
+    def _():
+        @pl.when(z < LATE)
+        def _():
+            pl.loop(z + 1, LATE)(arrive_and_answer)
+            pl.loop(LATE, NZ)(arrive)
+
+        @pl.when(z >= LATE)
+        def _():
+            pl.loop(z + 1, NZ)(arrive_and_answer)
+
+        plane_of(d_recv.at[NZ], NG - 1).wait()
+        pl.loop(0, z)(arrive)
+
+    pool(0)
+
+    @pl.when(z == 0)
+    def _():
+        pl.loop(SPAN, LATE)(arrive_and_answer)
+        pl.loop(LATE, 2 * SPAN)(arrive)
+
+    pool(1)
+
+    @pl.when(z == 0)
+    def _():
+        pl.loop(2 * SPAN, NZ)(arrive)
+
+    pool(2)
+
+    ng[f] = (acc[...] * scale).astype(BF)
     to_peers(ng, n_send, n_recv)
 
-    @pl.when(z < NZ - 1)
-    def _():
-        send_plane(NZ - 1)
-
+    @pl.when(z < LATE)
+    def _():
+        pl.loop(LATE, NZ)(send_plane)
+
+    peers_of(xg, x_recv).wait()
+    own_term = nn(w_v[:, 0:256], xg[...].reshape(NY * W, NODES)) + bias
     peers_of(ng, n_recv).wait()
     out = own_term + nn(w_v[:, 256:512], ng[...].reshape(NY * W, NODES))
     o_ref[...] = jnp.maximum(out, 0.0).astype(BF)
@@ -264,8 +319,9 @@
             V((1, 16), I32), V((16, 128), I32), V((16, 128), I32), V((8, 96), I32),
             V((NY, W, NODES), BF), V((NY, W, NODES), BF), V((NODES, 1024), BF),
             V((NODES, EDGES), BF), V((NODES + 16, EDGES), BF),
-            V((NODES, EDGES), BF), V((PART + 16, EDGES), BF),
-            V((NODES, NODES), BF), V((4 * PART * PARTS, NODES), BF), V((NZ * NX * 8, 256), BF),
+            V((NODES, EDGES // 2), BF), V((4 * HUB_PART + 16, EDGES // 2), BF),
+            V((NODES, NODES), BF), V((PART * PARTS, NODES), BF), V((NZ * NX * 8, 256), BF),
+            V((LINES, 256), BF), V((W, NODES), F32),
             V((NZ * NX, 8, 128), BF), V((NZ, NG, 8, 128), BF),
             DMA((11,)), pltpu.SemaphoreType.REGULAR, DMA(()), DMA(()), DMA(()), DMA(()),
             DMA((NZ + 1,)), DMA((NZ + 1,)),

time: 75.7 us -> 47.1 us (0.62)
  the two profiles are of different devices: /device:TPU:705 before, /device:TPU:648 now
where the time goes in v3:
time: 47.1 us; the launch traced here: 46.9 us
  Pallas kernels  45.5 us (97%)
  local copies, waits for them, and re-layouts  1.38 us (3%)
    pallas_call x1, Pallas kernels, shards(): pl.pallas_call(kernel, out_shape=jax.ShapeDtypeStruct((W, NODES), BF), in...  45.5 us
    unnamed x1, local copies, waits for them, and re-layouts  1.38 us

profile of v3, /device:TPU:648, one launch (start us, length us, event | category | flops | bytes accessed | tf_op | source)
XLA Modules:
  0.0 46.9 jit_solution(5470225404101800238)
XLA Ops:
  0.0 45.5 %shard_map.109 = bf16[32,512]{1,0:T(8,128)(2,1)} custom-call(bf16[32,512]{1,0:T(8,128)(2,1)} %bitcast.13, bf16[32,512]{1,0:T(8,128)(2,1)} %bitcast.14, bf16[1,32]{1,0:T(2,128)(2,1)} %bitcast.22, s32[16,128]{1,0:T(8,128)} %bitcast.15, s32[16,128]{1,0:T(8,128)} %bitcast.16, s32[1,16]{1,0:T(1,128)} %bitcast.23, s32[8,128]{1,0:T(8,128)} %bitcast.17, ...), custom_call_target="tpu_custom_call" | custom-call | tf_op jit(solution)/shard_map/pallas_call | solution.py:312
  45.5 1.4 %copy.13 = bf16[512,32]{0,1:T(8,128)(2,1)} copy(bf16[512,32]{0,1:T(8,128)(2,1)} %bitcast.12) | data formatting | bytes 65536

commit v4 on v1

v4 whole, which is shorter than its diff:
```python
import jax
import jax.numpy as jnp
from jax import lax
from jax.experimental import pallas as pl
from jax.experimental.pallas import tpu as pltpu
from jax.sharding import PartitionSpec as P

MESH = pl.DeviceIdType.MESH
BF = jnp.bfloat16
F32 = jnp.float32
NX, NZ, NY = 4, 12, 8
NQ = NX * NZ
NODES = 512
W = 32
EDGES = 2048
ROWS = NQ * 8
HUBS = NQ * 4
BNDS = NQ * 2
LINES = HUBS + BNDS


def nt(a, b):
    return lax.dot_general(a, b, (((1,), (1,)), ((), ())), preferred_element_type=F32)


def nn(a, b):
    return jnp.dot(a, b, preferred_element_type=F32)


def one_hot(row, size):
    at = lax.broadcasted_iota(jnp.int32, (size, row.shape[1]), 0)
    return jnp.where(at == row, 1.0, 0.0).astype(BF)


def kernel(
    x_hbm, w_hbm, b_hbm, ls_hbm, ld_hbm, hr_hbm, hs_hbm, hd_hbm, sr_hbm, bs_hbm, bd_hbm,
    o_ref,
    w_v, b_v, ls_v, ld_v, hr_v, es_v, ed_v, sr_v, xg, ot, ld1, ls1, ed1, es1, al, ar, pick, sel,
    sendb, recv, in_sem, ready, heard, all_in, y_send, y_recv, d_send, d_recv, c_send, c_recv,
):
    dom, f = lax.axis_index("dom"), lax.axis_index("feat")
    core = dom % 2
    q = dom // 2
    z, x = q % NZ, q // NZ

    def chip(xx, zz):
        return {"dom": (xx * NZ + zz) * 2 + core}

    sibling = {"dom": q * 2 + (1 - core)}

    rank = jnp.where(f <= NY // 2, jnp.maximum(2 * f - 1, 0), 2 * (NY - f))

    def at_rank(r):
        return {"feat": jnp.where(r % 2 == 1, (r + 1) // 2, lax.rem(NY - r // 2, NY))}

    def signal(sem, device_id):
        pl.semaphore_signal(sem, inc=1, device_id=device_id, device_id_type=MESH)

    loads = []
    for n, (src, dst) in enumerate((
        (x_hbm, xg.at[f]), (sr_hbm, sr_v), (hr_hbm, hr_v), (w_hbm, w_v), (b_hbm, b_v),
        (ls_hbm, ls_v), (ld_hbm, ld_v),
        (hs_hbm, es_v.at[pl.ds(0, 8)]), (bs_hbm, es_v.at[pl.ds(8, 8)]),
        (hd_hbm, ed_v.at[pl.ds(0, 8)]), (bd_hbm, ed_v.at[pl.ds(8, 8)]),
    )):
        copy = pltpu.make_async_copy(src, dst, in_sem.at[n])
        copy.start()
        loads.append(copy)

    barrier = pltpu.get_barrier_semaphore()
    signal(barrier, sibling)

    @pl.loop(rank + 1, NY)
    def _(r):
        signal(barrier, at_rank(r))

    @pl.when(z == 0)
    def _():
        for dx in range(1, NX):
            signal(barrier, chip(lax.rem(x + dx, NX), 0))

        @pl.loop(1, NZ)
        def _(zz):
            for xx in range(NX):
                signal(barrier, chip(xx, zz))

    pl.semaphore_wait(barrier, 1 + rank + jnp.where(z == 0, NX - 1, NX))

    @pl.when(z > 0)
    def _():
        for xx in range(NX):
            signal(heard, chip(xx, 0))

    @pl.loop(0, rank)
    def _(r):
        signal(ready.at[rank], at_rank(r))

    def send_x(r):
        pltpu.make_async_remote_copy(
            src_ref=xg.at[f], dst_ref=xg.at[f], send_sem=y_send, recv_sem=y_recv,
            device_id=at_rank(r), device_id_type=MESH,
        ).start()

    loads[0].wait()
    pl.loop(0, rank)(send_x)
    for copy in loads[1:]:
        copy.wait()

    lane = lax.broadcasted_iota(jnp.int32, (16, 512), 1)
    hub = lax.broadcasted_iota(jnp.int32, (16, 512), 0)
    spread = jnp.where(
        (lane // 128 == hub % 4) & (lane % 128 == 96 + hub // 4), 1.0, 0.0
    ).astype(BF)
    hub_lanes = nn(one_hot(hr_v[...], NODES), spread)
    for c in range(8):
        part = one_hot(sr_v[c : c + 1, :], NODES)
        part = jnp.concatenate([part, jnp.zeros((NODES, 32), BF)], axis=1)
        j, si = c % 4, c // 4
        if si == 0:
            part = part + hub_lanes[:, j * 128 : j * 128 + 128].astype(BF)
        ot[:, j * 256 + si * 128 : j * 256 + si * 128 + 128] = part
    row = lax.broadcasted_iota(jnp.int32, (ROWS, 256), 0)
    col = lax.broadcasted_iota(jnp.int32, (ROWS, 256), 1)
    t = row % 8
    want = jnp.where(t < 4, (t % 2) * 128 + (row // 8) * 2 + t // 2, 92 + t)
    pick[...] = jnp.where(col == want, 1.0, 0.0).astype(BF)
    line = lax.broadcasted_iota(jnp.int32, (ROWS, LINES), 0)
    at = lax.broadcasted_iota(jnp.int32, (ROWS, LINES), 1)
    low = at - HUBS
    want = jnp.where(low < 0, (at // 4) * 8 + 4 + at % 4, (low // 2) * 8 + 2 * core + low % 2)
    sel[...] = jnp.where(line == want, 1.0, 0.0).astype(BF)

    def hot_rows(ref, at, out, size, first=0):
        @pl.loop(0, out.shape[1] // 128)
        def _(i):
            lanes = pl.ds(pl.multiple_of(i * 128, 128), 128)
            out[0:size, lanes] = one_hot(ref[pl.ds(first + i, 1), :] - at, size)

    ls1[NODES : NODES + 16, :] = jnp.ones((16, EDGES), BF)
    es1[4 * HUBS : 4 * HUBS + 16, :] = jnp.ones((16, EDGES // 2), BF)
    hot_rows(ls_v, 0, ls1, NODES)
    hot_rows(ld_v, 0, ld1, NODES)
    counts = nt(ls1[...], ld1[...])
    al[...] = counts[:NODES].astype(BF)
    degree = counts[NODES : NODES + 1]

    @pl.loop(rank + 1, NY)
    def _(r):
        pl.semaphore_wait(ready.at[r], 1)
        send_x(r)

    h = es_v[0:8, :]
    s = h // 16
    es_v[0:8, :] = (s % 2) * (4 * HUBS) + (h % 4) * HUBS + (s // 2) * 4 + (h // 4) % 4
    b = es_v[8:16, :]
    s = b // 8
    es_v[8:16, :] = (s % 2) * (4 * BNDS) + (b % 4) * BNDS + (s // 2) * 2 + (b // 4) % 2

    hot_rows(ed_v, 0, ed1, NODES)
    for side in range(2):
        hot_rows(es_v, side * (4 * HUBS), es1, 4 * HUBS)
        got = nt(es1[...], ed1[...])
        for j in range(4):
            base = (side * 4 + j) * LINES
            ar[base : base + HUBS, :] = got[j * HUBS : (j + 1) * HUBS].astype(BF)
    degree = degree + got[4 * HUBS : 4 * HUBS + 1]
    hot_rows(ed_v, 0, ed1, NODES, 8)
    for side in range(2):
        hot_rows(es_v, side * (4 * BNDS), es1, 4 * BNDS, 8)
        got = nt(es1[0 : 4 * BNDS, :], ed1[...])
        for j in range(4):
            base = (side * 4 + j) * LINES + HUBS
            ar[base : base + BNDS, :] = got[j * BNDS : (j + 1) * BNDS].astype(BF)
    degree = degree + nt(es1[4 * HUBS : 4 * HUBS + 16, :], ed1[...])[0:1]
    scale = 1.0 / jnp.maximum(degree, 1.0)
    diag = lax.broadcasted_iota(jnp.int32, (W, W), 0) == lax.broadcasted_iota(jnp.int32, (W, W), 1)
    bias = jnp.sum(jnp.where(diag, b_v[...].astype(F32), 0.0), axis=1, keepdims=True)
    eye = jnp.where(
        lax.broadcasted_iota(jnp.int32, (128, 128), 0)
        == lax.broadcasted_iota(jnp.int32, (128, 128), 1), 1.0, 0.0,
    ).astype(BF)

    def all_of(region, sem):
        return pltpu.make_async_copy(region, region, sem)

    others = xg.at[pl.ds(0, NY - 1)]
    all_of(others, y_recv).wait()

    both = jnp.concatenate([w_v[:, 256:512], w_v[:, 0:256]], axis=0)
    yz = nn(both, xg[...].reshape(NY * W, NODES))
    high = yz[0:W].astype(BF)
    lists = jnp.concatenate(
        [nn(high, ot[:, j * 256 : j * 256 + 256]) for j in range(4)], axis=0
    ).astype(BF)
    sendb[...] = nt(pick[...], lists).reshape(NQ, 8, 128).astype(BF)
    recv[core, q] = sendb[q]

    @pl.when(z == 0)
    def _():
        pl.semaphore_wait(heard, NX * (NZ - 1))

        @pl.when(x > 0)
        def _():
            @pl.loop(0, NZ - 1)
            def _(i):
                zz = lax.rem(i + 5, NZ - 1) + 1
                signal(all_in, chip(x, zz))

                @pl.when(x == 1)
                def _():
                    signal(all_in, chip(0, zz))

    @pl.when(z > 0)
    def _():
        pl.semaphore_wait(all_in, 1)

    def send_rows_to(xx, zz):
        pltpu.make_async_remote_copy(
            src_ref=sendb.at[xx * NZ + zz], dst_ref=recv.at[core, q], send_sem=d_send,
            recv_sem=d_recv, device_id=chip(xx, zz), device_id_type=MESH,
        ).start()

    @pl.loop(0, NZ)
    def _(zz):
        for dx in range(1, NX):
            send_rows_to(lax.rem(x + dx, NX), zz)

        @pl.when(zz != z)
        def _():
            send_rows_to(x, zz)

    low_y = (yz[0:W] - high.astype(F32)).astype(BF)
    near = nn(jnp.concatenate([high, low_y], axis=0), al[...])
    pooled = near[0:W] + near[W : 2 * W]

    def add_half(side):
        rows = recv[side].reshape(ROWS, 128)
        turned = nn(nt(eye, rows).astype(BF), sel[...]).astype(BF)
        wide = jnp.concatenate([turned[j * W : j * W + W] for j in range(4)], axis=1)
        return nn(wide, ar[pl.ds(pl.multiple_of(side * (4 * LINES), 16), 4 * LINES), :])

    rest = recv.at[0, pl.ds(0, NQ - 1)]
    all_of(rest, d_recv).wait()
    swap = pltpu.make_async_remote_copy(
        src_ref=recv.at[core], dst_ref=recv.at[core], send_sem=c_send, recv_sem=c_recv,
        device_id=sibling, device_id_type=MESH,
    )
    swap.start()
    pooled = pooled + add_half(core)
    swap.wait_recv()
    pooled = pooled + add_half(1 - core)

    out = yz[W : 2 * W] + bias + pooled * scale
    o_ref[...] = jnp.maximum(out, 0.0).astype(BF)
    all_of(others, y_send).wait()
    all_of(rest, d_send).wait()
    swap.wait_send()


def shards(
    features, weight, bias, local_src, local_dst, hub_rows, hub_src, hub_dst, send_rows,
    bnd_src, bnd_dst,
):
    V = pltpu.VMEM
    I32 = jnp.int32
    DMA = pltpu.SemaphoreType.DMA
    REGULAR = pltpu.SemaphoreType.REGULAR
    out = pl.pallas_call(
        kernel,
        out_shape=jax.ShapeDtypeStruct((W, NODES), BF),
        in_specs=[pl.BlockSpec(memory_space=pl.ANY)] * 11,
        out_specs=pl.BlockSpec(memory_space=pltpu.VMEM),
        scratch_shapes=[
            V((W, NODES), BF), V((1, W), BF), V((16, 128), I32), V((16, 128), I32),
            V((1, 16), I32), V((16, 128), I32), V((16, 128), I32), V((8, 96), I32),
            V((NY, W, NODES), BF), V((NODES, 1024), BF),
            V((NODES, EDGES), BF), V((NODES + 16, EDGES), BF),
            V((NODES, EDGES // 2), BF), V((4 * HUBS + 16, EDGES // 2), BF),
            V((NODES, NODES), BF), V((8 * LINES, NODES), BF), V((ROWS, 256), BF),
            V((ROWS, LINES), BF), V((NQ, 8, 128), BF), V((2, NQ, 8, 128), BF),
            DMA((11,)), REGULAR((NY,)), REGULAR, REGULAR, DMA(()), DMA(()), DMA(()), DMA(()),
            DMA(()), DMA(()),
        ],
        compiler_params=pltpu.CompilerParams(
            collective_id=0, has_side_effects=True, vmem_limit_bytes=56 * 1024 * 1024
        ),
    )(
        features.T, weight.T, bias.reshape(1, W),
        local_src.reshape(16, 128), local_dst.reshape(16, 128), hub_rows.reshape(1, 16),
        hub_src.reshape(8, 128), hub_dst.reshape(8, 128), send_rows.T,
        bnd_src.reshape(8, 128), bnd_dst.reshape(8, 128),
    )
    return out.T


def solution(mesh):
    return jax.shard_map(
        shards,
        mesh=mesh,
        in_specs=(
            P("dom", "feat"), P(None, "feat"), P("feat"), P("dom"), P("dom"), P("dom"),
            P("dom"), P("dom"), P("dom", None), P("dom"), P("dom"),
        ),
        out_specs=P("dom", "feat"),
        check_vma=False,
    )
```

time: 41 us -> 38.5 us (0.939)
  Pallas kernels: 39.3 us -> 36.8 us
    pallas_call x1, Pallas kernels: 39.3 us -> 36.8 us  [shards(): pl.pallas_call(kernel, out_shape=jax.ShapeDtypeStruct((W, NODES), BF), in...]
where the time goes in v4:
time: 38.5 us; the launch traced here: 38.2 us
  Pallas kernels  36.8 us (96%)
  local copies, waits for them, and re-layouts  1.38 us (4%)
    pallas_call x1, Pallas kernels, shards(): pl.pallas_call(kernel, out_shape=jax.ShapeDtypeStruct((W, NODES), BF), in...  36.8 us
    unnamed x1, local copies, waits for them, and re-layouts  1.38 us

profile of v4, /device:TPU:1, one launch (start us, length us, event | category | flops | bytes accessed | tf_op | source)
XLA Modules:
  0.0 38.2 jit_solution(10748051735758009987)
XLA Ops:
  0.0 36.8 %shard_map.109 = bf16[32,512]{1,0:T(8,128)(2,1)} custom-call(bf16[32,512]{1,0:T(8,128)(2,1)} %bitcast.13, bf16[32,512]{1,0:T(8,128)(2,1)} %bitcast.14, bf16[1,32]{1,0:T(2,128)(2,1)} %bitcast.22, s32[16,128]{1,0:T(8,128)} %bitcast.15, s32[16,128]{1,0:T(8,128)} %bitcast.16, s32[1,16]{1,0:T(1,128)} %bitcast.23, s32[8,128]{1,0:T(8,128)} %bitcast.17, ...), custom_call_target="tpu_custom_call" | custom-call | tf_op jit(solution)/shard_map/pallas_call | solution.py:268
  36.9 1.4 %copy.13 = bf16[512,32]{0,1:T(8,128)(2,1)} copy(bf16[512,32]{0,1:T(8,128)(2,1)} %bitcast.12) | data formatting | bytes 65536

commit v5 on v4

--- a/solution.py
+++ b/solution.py
@@ -17,6 +17,8 @@
 HUBS = NQ * 4
 BNDS = NQ * 2
 LINES = HUBS + BNDS
+DIRECT = 3
+Y_ORDER = (4, 3, 5, 2, 6, 1, 7)
 
 
 def nt(a, b):
@@ -36,22 +38,21 @@
     x_hbm, w_hbm, b_hbm, ls_hbm, ld_hbm, hr_hbm, hs_hbm, hd_hbm, sr_hbm, bs_hbm, bd_hbm,
     o_ref,
     w_v, b_v, ls_v, ld_v, hr_v, es_v, ed_v, sr_v, xg, ot, ld1, ls1, ed1, es1, al, ar, pick, sel,
-    sendb, recv, in_sem, ready, heard, all_in, y_send, y_recv, d_send, d_recv, c_send, c_recv,
+    sendb, recv, in_sem, heard, all_in, y_send, y_recv, d_send, d_recv, c_send, c_recv,
 ):
     dom, f = lax.axis_index("dom"), lax.axis_index("feat")
     core = dom % 2
     q = dom // 2
     z, x = q % NZ, q // NZ
 
-    def chip(xx, zz):
-        return {"dom": (xx * NZ + zz) * 2 + core}
-
-    sibling = {"dom": q * 2 + (1 - core)}
-
-    rank = jnp.where(f <= NY // 2, jnp.maximum(2 * f - 1, 0), 2 * (NY - f))
-
-    def at_rank(r):
-        return {"feat": jnp.where(r % 2 == 1, (r + 1) // 2, lax.rem(NY - r // 2, NY))}
+    def chip(xx, zz, on=core):
+        return {"dom": (xx * NZ + zz) * 2 + on}
+
+    other = 1 - core
+    sibling = chip(x, z, other)
+
+    def peer(i):
+        return {"feat": lax.rem(f + i, NY)}
 
     def signal(sem, device_id):
         pl.semaphore_signal(sem, inc=1, device_id=device_id, device_id_type=MESH)
@@ -68,41 +69,36 @@
         loads.append(copy)
 
     barrier = pltpu.get_barrier_semaphore()
+    for i in Y_ORDER:
+        signal(barrier, peer(i))
     signal(barrier, sibling)
 
-    @pl.loop(rank + 1, NY)
-    def _(r):
-        signal(barrier, at_rank(r))
-
     @pl.when(z == 0)
     def _():
         for dx in range(1, NX):
-            signal(barrier, chip(lax.rem(x + dx, NX), 0))
-
-        @pl.loop(1, NZ)
-        def _(zz):
+            for on in range(2):
+                signal(barrier, chip(lax.rem(x + dx, NX), 0, on))
+
+        @pl.loop(0, NZ - 1)
+        def _(i):
             for xx in range(NX):
-                signal(barrier, chip(xx, zz))
-
-    pl.semaphore_wait(barrier, 1 + rank + jnp.where(z == 0, NX - 1, NX))
+                for on in range(2):
+                    signal(barrier, chip(xx, lax.rem(i + 5, NZ - 1) + 1, on))
+
+    pl.semaphore_wait(barrier, NY + jnp.where(z == 0, 2 * NX - 2, 2 * NX))
+
+    loads[0].wait()
+    for i in Y_ORDER:
+        pltpu.make_async_remote_copy(
+            src_ref=xg.at[f], dst_ref=xg.at[f], send_sem=y_send, recv_sem=y_recv,
+            device_id=peer(i), device_id_type=MESH,
+        ).start()
 
     @pl.when(z > 0)
     def _():
         for xx in range(NX):
             signal(heard, chip(xx, 0))
 
-    @pl.loop(0, rank)
-    def _(r):
-        signal(ready.at[rank], at_rank(r))
-
-    def send_x(r):
-        pltpu.make_async_remote_copy(
-            src_ref=xg.at[f], dst_ref=xg.at[f], send_sem=y_send, recv_sem=y_recv,
-            device_id=at_rank(r), device_id_type=MESH,
-        ).start()
-
-    loads[0].wait()
-    pl.loop(0, rank)(send_x)
     for copy in loads[1:]:
         copy.wait()
 
@@ -144,11 +140,6 @@
     al[...] = counts[:NODES].astype(BF)
     degree = counts[NODES : NODES + 1]
 
-    @pl.loop(rank + 1, NY)
-    def _(r):
-        pl.semaphore_wait(ready.at[r], 1)
-        send_x(r)
-
     h = es_v[0:8, :]
     s = h // 16
     es_v[0:8, :] = (s % 2) * (4 * HUBS) + (h % 4) * HUBS + (s // 2) * 4 + (h // 4) % 4
@@ -164,6 +155,77 @@
             base = (side * 4 + j) * LINES
             ar[base : base + HUBS, :] = got[j * HUBS : (j + 1) * HUBS].astype(BF)
     degree = degree + got[4 * HUBS : 4 * HUBS + 1]
+    diag = lax.broadcasted_iota(jnp.int32, (W, W), 0) == lax.broadcasted_iota(jnp.int32, (W, W), 1)
+    bias = jnp.sum(jnp.where(diag, b_v[...].astype(F32), 0.0), axis=1, keepdims=True)
+    eye = jnp.where(
+        lax.broadcasted_iota(jnp.int32, (128, 128), 0)
+        == lax.broadcasted_iota(jnp.int32, (128, 128), 1), 1.0, 0.0,
+    ).astype(BF)
+
+    def all_of(region, sem):
+        return pltpu.make_async_copy(region, region, sem)
+
+    others = xg.at[pl.ds(0, NY - 1)]
+    all_of(others, y_recv).wait()
+
+    both = jnp.concatenate([w_v[:, 256:512], w_v[:, 0:256]], axis=0)
+    yz = nn(both, xg[...].reshape(NY * W, NODES))
+    high = yz[0:W].astype(BF)
+    lists = jnp.concatenate(
+        [nn(high, ot[:, j * 256 : j * 256 + 256]) for j in range(4)], axis=0
+    ).astype(BF)
+    sendb[...] = nt(pick[...], lists).reshape(NQ, 8, 128).astype(BF)
+    recv[core, q] = sendb[q]
+
+    @pl.when(z == 0)
+    def _():
+        pl.semaphore_wait(heard, NX * (NZ - 1))
+
+        @pl.when(x > 0)
+        def _():
+            @pl.loop(0, NZ - 1)
+            def _(i):
+                zz = lax.rem(i + 5, NZ - 1) + 1
+                signal(all_in, chip(x, zz))
+
+                @pl.when(x == 1)
+                def _():
+                    signal(all_in, chip(0, zz))
+
+    def send_rows_to(xx, zz, on=core):
+        pltpu.make_async_remote_copy(
+            src_ref=sendb.at[xx * NZ + zz], dst_ref=recv.at[core, q], send_sem=d_send.at[0],
+            recv_sem=d_recv.at[0], device_id=chip(xx, zz, on), device_id_type=MESH,
+        ).start()
+
+    def send_across(xx, zz):
+        pltpu.make_async_remote_copy(
+            src_ref=sendb.at[xx * NZ + zz], dst_ref=recv.at[core, q], send_sem=d_send.at[1],
+            recv_sem=d_recv.at[1], device_id=chip(xx, zz, other), device_id_type=MESH,
+        ).start()
+
+    def send_plane(zz):
+        for dx in range(1, NX):
+            send_rows_to(lax.rem(x + dx, NX), zz)
+
+        @pl.when(zz != z)
+        def _():
+            send_rows_to(x, zz)
+
+    def send_first_plane(zz):
+        send_plane(zz)
+        for xx in range(NX):
+            send_across(xx, zz)
+
+    send_first_plane(0)
+
+    @pl.when(z > 0)
+    def _():
+        pl.semaphore_wait(all_in, 1)
+
+    pl.loop(1, DIRECT)(send_first_plane)
+    pl.loop(DIRECT, NZ)(send_plane)
+
     hot_rows(ed_v, 0, ed1, NODES, 8)
     for side in range(2):
         hot_rows(es_v, side * (4 * BNDS), es1, 4 * BNDS, 8)
@@ -173,62 +235,6 @@
             ar[base : base + BNDS, :] = got[j * BNDS : (j + 1) * BNDS].astype(BF)
     degree = degree + nt(es1[4 * HUBS : 4 * HUBS + 16, :], ed1[...])[0:1]
     scale = 1.0 / jnp.maximum(degree, 1.0)
-    diag = lax.broadcasted_iota(jnp.int32, (W, W), 0) == lax.broadcasted_iota(jnp.int32, (W, W), 1)
-    bias = jnp.sum(jnp.where(diag, b_v[...].astype(F32), 0.0), axis=1, keepdims=True)
-    eye = jnp.where(
-        lax.broadcasted_iota(jnp.int32, (128, 128), 0)
-        == lax.broadcasted_iota(jnp.int32, (128, 128), 1), 1.0, 0.0,
-    ).astype(BF)
-
-    def all_of(region, sem):
-        return pltpu.make_async_copy(region, region, sem)
-
-    others = xg.at[pl.ds(0, NY - 1)]
-    all_of(others, y_recv).wait()
-
-    both = jnp.concatenate([w_v[:, 256:512], w_v[:, 0:256]], axis=0)
-    yz = nn(both, xg[...].reshape(NY * W, NODES))
-    high = yz[0:W].astype(BF)
-    lists = jnp.concatenate(
-        [nn(high, ot[:, j * 256 : j * 256 + 256]) for j in range(4)], axis=0
-    ).astype(BF)
-    sendb[...] = nt(pick[...], lists).reshape(NQ, 8, 128).astype(BF)
-    recv[core, q] = sendb[q]
-
-    @pl.when(z == 0)
-    def _():
-        pl.semaphore_wait(heard, NX * (NZ - 1))
-
-        @pl.when(x > 0)
-        def _():
-            @pl.loop(0, NZ - 1)
-            def _(i):
-                zz = lax.rem(i + 5, NZ - 1) + 1
-                signal(all_in, chip(x, zz))
-
-                @pl.when(x == 1)
-                def _():
-                    signal(all_in, chip(0, zz))
-
-    @pl.when(z > 0)
-    def _():
-        pl.semaphore_wait(all_in, 1)
-
-    def send_rows_to(xx, zz):
-        pltpu.make_async_remote_copy(
-            src_ref=sendb.at[xx * NZ + zz], dst_ref=recv.at[core, q], send_sem=d_send,
-            recv_sem=d_recv, device_id=chip(xx, zz), device_id_type=MESH,
-        ).start()
-
-    @pl.loop(0, NZ)
-    def _(zz):
-        for dx in range(1, NX):
-            send_rows_to(lax.rem(x + dx, NX), zz)
-
-        @pl.when(zz != z)
-        def _():
-            send_rows_to(x, zz)
-
     low_y = (yz[0:W] - high.astype(F32)).astype(BF)
     near = nn(jnp.concatenate([high, low_y], axis=0), al[...])
     pooled = near[0:W] + near[W : 2 * W]
@@ -240,21 +246,33 @@
         return nn(wide, ar[pl.ds(pl.multiple_of(side * (4 * LINES), 16), 4 * LINES), :])
 
     rest = recv.at[0, pl.ds(0, NQ - 1)]
-    all_of(rest, d_recv).wait()
+    all_of(rest, d_recv.at[0]).wait()
     swap = pltpu.make_async_remote_copy(
         src_ref=recv.at[core], dst_ref=recv.at[core], send_sem=c_send, recv_sem=c_recv,
         device_id=sibling, device_id_type=MESH,
     )
-    swap.start()
+    pl.when(z >= DIRECT)(swap.start)
     pooled = pooled + add_half(core)
-    swap.wait_recv()
-    pooled = pooled + add_half(1 - core)
+
+    @pl.when(z >= DIRECT)
+    def _():
+        swap.wait_recv()
+
+    @pl.when(z < DIRECT)
+    def _():
+        all_of(recv.at[0], d_recv.at[1]).wait()
+
+    pooled = pooled + add_half(other)
 
     out = yz[W : 2 * W] + bias + pooled * scale
     o_ref[...] = jnp.maximum(out, 0.0).astype(BF)
     all_of(others, y_send).wait()
-    all_of(rest, d_send).wait()
-    swap.wait_send()
+    all_of(rest, d_send.at[0]).wait()
+    all_of(recv.at[0, pl.ds(0, NX * DIRECT)], d_send.at[1]).wait()
+
+    @pl.when(z >= DIRECT)
+    def _():
+        swap.wait_send()
 
 
 def shards(
@@ -278,7 +296,7 @@
             V((NODES, EDGES // 2), BF), V((4 * HUBS + 16, EDGES // 2), BF),
             V((NODES, NODES), BF), V((8 * LINES, NODES), BF), V((ROWS, 256), BF),
             V((ROWS, LINES), BF), V((NQ, 8, 128), BF), V((2, NQ, 8, 128), BF),
-            DMA((11,)), REGULAR((NY,)), REGULAR, REGULAR, DMA(()), DMA(()), DMA(()), DMA(()),
+            DMA((11,)), REGULAR, REGULAR, DMA(()), DMA(()), DMA((2,)), DMA((2,)),
             DMA(()), DMA(()),
         ],
         compiler_params=pltpu.CompilerParams(

time: 38.5 us -> 36.8 us (0.956)
  the two profiles are of different devices: /device:TPU:1 before, /device:TPU:193 now
where the time goes in v5:
time: 36.8 us; the launch traced here: 36.6 us
  Pallas kernels  35.2 us (96%)
  local copies, waits for them, and re-layouts  1.38 us (4%)
    pallas_call x1, Pallas kernels, shards(): pl.pallas_call(kernel, out_shape=jax.ShapeDtypeStruct((W, NODES), BF), in...  35.2 us
    unnamed x1, local copies, waits for them, and re-layouts  1.38 us

profile of v5, /device:TPU:193, one launch (start us, length us, event | category | flops | bytes accessed | tf_op | source)
XLA Modules:
  0.0 36.6 jit_solution(18054714711387254757)
XLA Ops:
  0.0 35.2 %shard_map.109 = bf16[32,512]{1,0:T(8,128)(2,1)} custom-call(bf16[32,512]{1,0:T(8,128)(2,1)} %bitcast.13, bf16[32,512]{1,0:T(8,128)(2,1)} %bitcast.14, bf16[1,32]{1,0:T(2,128)(2,1)} %bitcast.22, s32[16,128]{1,0:T(8,128)} %bitcast.15, s32[16,128]{1,0:T(8,128)} %bitcast.16, s32[1,16]{1,0:T(1,128)} %bitcast.23, s32[8,128]{1,0:T(8,128)} %bitcast.17, ...), custom_call_target="tpu_custom_call" | custom-call | tf_op jit(solution)/shard_map/pallas_call | solution.py:286
  35.2 1.4 %copy.13 = bf16[512,32]{0,1:T(8,128)(2,1)} copy(bf16[512,32]{0,1:T(8,128)(2,1)} %bitcast.12) | data formatting | bytes 65536

commit v6 on v5

--- a/solution.py
+++ b/solution.py
@@ -17,7 +17,7 @@
 HUBS = NQ * 4
 BNDS = NQ * 2
 LINES = HUBS + BNDS
-DIRECT = 3
+EARLY = 6
 Y_ORDER = (4, 3, 5, 2, 6, 1, 7)
 
 
@@ -37,8 +37,8 @@
 def kernel(
     x_hbm, w_hbm, b_hbm, ls_hbm, ld_hbm, hr_hbm, hs_hbm, hd_hbm, sr_hbm, bs_hbm, bd_hbm,
     o_ref,
-    w_v, b_v, ls_v, ld_v, hr_v, es_v, ed_v, sr_v, xg, ot, ld1, ls1, ed1, es1, al, ar, pick, sel,
-    sendb, recv, in_sem, heard, all_in, y_send, y_recv, d_send, d_recv, c_send, c_recv,
+    w_v, b_v, ls_v, ld_v, hr_v, es_v, ed_v, sr_v, xg, ng, ot, ld1, ls1, ed1, es1, al, ar, pick, sel,
+    sendb, recv, in_sem, ready, heard, all_in, y_send, y_recv, d_send, d_recv, c_send, c_recv,
 ):
     dom, f = lax.axis_index("dom"), lax.axis_index("feat")
     core = dom % 2
@@ -68,38 +68,31 @@
         copy.start()
         loads.append(copy)
 
+    rank = jnp.where(f <= NY // 2, jnp.maximum(2 * f - 1, 0), 2 * (NY - f))
+
+    def at_rank(r):
+        return {"feat": jnp.where(r % 2 == 1, (r + 1) // 2, lax.rem(NY - r // 2, NY))}
+
     barrier = pltpu.get_barrier_semaphore()
-    for i in Y_ORDER:
-        signal(barrier, peer(i))
+
+    @pl.loop(rank + 1, NY)
+    def _(r):
+        signal(barrier, at_rank(r))
+
     signal(barrier, sibling)
-
-    @pl.when(z == 0)
-    def _():
-        for dx in range(1, NX):
-            for on in range(2):
-                signal(barrier, chip(lax.rem(x + dx, NX), 0, on))
-
-        @pl.loop(0, NZ - 1)
-        def _(i):
+    for dx in range(1, NX):
+        for on in range(2):
+            signal(barrier, chip(lax.rem(x + dx, NX), z, on))
+
+    @pl.when(z < EARLY)
+    def _():
+        @pl.loop(z + 1, NZ)
+        def _(zz):
             for xx in range(NX):
                 for on in range(2):
-                    signal(barrier, chip(xx, lax.rem(i + 5, NZ - 1) + 1, on))
-
-    pl.semaphore_wait(barrier, NY + jnp.where(z == 0, 2 * NX - 2, 2 * NX))
-
-    loads[0].wait()
-    for i in Y_ORDER:
-        pltpu.make_async_remote_copy(
-            src_ref=xg.at[f], dst_ref=xg.at[f], send_sem=y_send, recv_sem=y_recv,
-            device_id=peer(i), device_id_type=MESH,
-        ).start()
-
-    @pl.when(z > 0)
-    def _():
-        for xx in range(NX):
-            signal(heard, chip(xx, 0))
-
-    for copy in loads[1:]:
+                    signal(barrier, chip(xx, zz, on))
+
+    for copy in loads:
         copy.wait()
 
     lane = lax.broadcasted_iota(jnp.int32, (16, 512), 1)
@@ -126,6 +119,60 @@
     want = jnp.where(low < 0, (at // 4) * 8 + 4 + at % 4, (low // 2) * 8 + 2 * core + low % 2)
     sel[...] = jnp.where(line == want, 1.0, 0.0).astype(BF)
 
+    def all_of(region, sem):
+        return pltpu.make_async_copy(region, region, sem)
+
+    own = xg[f]
+    lists = jnp.concatenate(
+        [nn(own, ot[:, j * 256 : j * 256 + 256]) for j in range(4)], axis=0
+    ).astype(BF)
+    sendb[...] = nt(pick[...], lists).reshape(NQ, 8, 128).astype(BF)
+
+    def send_rows_to(xx, zz):
+        pltpu.make_async_remote_copy(
+            src_ref=sendb.at[xx * NZ + zz], dst_ref=recv.at[core, q], send_sem=d_send.at[0],
+            recv_sem=d_recv.at[0], device_id=chip(xx, zz), device_id_type=MESH,
+        ).start()
+
+    def send_across(xx, zz):
+        pltpu.make_async_remote_copy(
+            src_ref=sendb.at[xx * NZ + zz], dst_ref=recv.at[core, q], send_sem=d_send.at[1],
+            recv_sem=d_recv.at[1], device_id=chip(xx, zz, other), device_id_type=MESH,
+        ).start()
+
+    def send_plane(zz):
+        for dx in range(1, NX):
+            send_rows_to(lax.rem(x + dx, NX), zz)
+
+        @pl.when(zz != z)
+        def _():
+            send_rows_to(x, zz)
+
+    def send_early_plane(zz):
+        send_plane(zz)
+        for xx in range(NX):
+            send_across(xx, zz)
+
+    pl.semaphore_wait(barrier, rank + 2 * NX - 1 + 2 * NX * jnp.minimum(z, EARLY))
+
+    @pl.when(z > 0)
+    def _():
+        for xx in range(NX):
+            signal(heard, chip(xx, 0))
+
+    pl.loop(0, jnp.minimum(z + 1, EARLY))(send_early_plane)
+
+    @pl.when(z >= EARLY)
+    def _():
+        for dx in range(1, NX):
+            send_rows_to(lax.rem(x + dx, NX), z)
+
+    @pl.loop(0, rank)
+    def _(r):
+        signal(ready, at_rank(r))
+
+    recv[core, q] = sendb[q]
+
     def hot_rows(ref, at, out, size, first=0):
         @pl.loop(0, out.shape[1] // 128)
         def _(i):
@@ -139,6 +186,21 @@
     counts = nt(ls1[...], ld1[...])
     al[...] = counts[:NODES].astype(BF)
     degree = counts[NODES : NODES + 1]
+
+    def to_peers(block, n):
+        for i in Y_ORDER:
+            pltpu.make_async_remote_copy(
+                src_ref=block.at[f], dst_ref=block.at[f], send_sem=y_send.at[n],
+                recv_sem=y_recv.at[n], device_id=peer(i), device_id_type=MESH,
+            ).start()
+
+    others = xg.at[pl.ds(0, NY - 1)]
+
+    @pl.when(rank < NY - 1)
+    def _():
+        pl.semaphore_wait(ready, NY - 1 - rank)
+
+    to_peers(xg, 0)
 
     h = es_v[0:8, :]
     s = h // 16
@@ -155,28 +217,6 @@
             base = (side * 4 + j) * LINES
             ar[base : base + HUBS, :] = got[j * HUBS : (j + 1) * HUBS].astype(BF)
     degree = degree + got[4 * HUBS : 4 * HUBS + 1]
-    diag = lax.broadcasted_iota(jnp.int32, (W, W), 0) == lax.broadcasted_iota(jnp.int32, (W, W), 1)
-    bias = jnp.sum(jnp.where(diag, b_v[...].astype(F32), 0.0), axis=1, keepdims=True)
-    eye = jnp.where(
-        lax.broadcasted_iota(jnp.int32, (128, 128), 0)
-        == lax.broadcasted_iota(jnp.int32, (128, 128), 1), 1.0, 0.0,
-    ).astype(BF)
-
-    def all_of(region, sem):
-        return pltpu.make_async_copy(region, region, sem)
-
-    others = xg.at[pl.ds(0, NY - 1)]
-    all_of(others, y_recv).wait()
-
-    both = jnp.concatenate([w_v[:, 256:512], w_v[:, 0:256]], axis=0)
-    yz = nn(both, xg[...].reshape(NY * W, NODES))
-    high = yz[0:W].astype(BF)
-    lists = jnp.concatenate(
-        [nn(high, ot[:, j * 256 : j * 256 + 256]) for j in range(4)], axis=0
-    ).astype(BF)
-    sendb[...] = nt(pick[...], lists).reshape(NQ, 8, 128).astype(BF)
-    recv[core, q] = sendb[q]
-
     @pl.when(z == 0)
     def _():
         pl.semaphore_wait(heard, NX * (NZ - 1))
@@ -192,39 +232,18 @@
                 def _():
                     signal(all_in, chip(0, zz))
 
-    def send_rows_to(xx, zz, on=core):
-        pltpu.make_async_remote_copy(
-            src_ref=sendb.at[xx * NZ + zz], dst_ref=recv.at[core, q], send_sem=d_send.at[0],
-            recv_sem=d_recv.at[0], device_id=chip(xx, zz, on), device_id_type=MESH,
-        ).start()
-
-    def send_across(xx, zz):
-        pltpu.make_async_remote_copy(
-            src_ref=sendb.at[xx * NZ + zz], dst_ref=recv.at[core, q], send_sem=d_send.at[1],
-            recv_sem=d_recv.at[1], device_id=chip(xx, zz, other), device_id_type=MESH,
-        ).start()
-
-    def send_plane(zz):
-        for dx in range(1, NX):
-            send_rows_to(lax.rem(x + dx, NX), zz)
-
+    @pl.when(z > 0)
+    def _():
+        pl.semaphore_wait(all_in, 1)
+
+    pl.loop(jnp.minimum(z + 1, EARLY), EARLY)(send_early_plane)
+
+    @pl.loop(EARLY, NZ)
+    def _(zz):
         @pl.when(zz != z)
         def _():
-            send_rows_to(x, zz)
-
-    def send_first_plane(zz):
-        send_plane(zz)
-        for xx in range(NX):
-            send_across(xx, zz)
-
-    send_first_plane(0)
-
-    @pl.when(z > 0)
-    def _():
-        pl.semaphore_wait(all_in, 1)
-
-    pl.loop(1, DIRECT)(send_first_plane)
-    pl.loop(DIRECT, NZ)(send_plane)
+            for xx in range(NX):
+                send_rows_to(xx, zz)
 
     hot_rows(ed_v, 0, ed1, NODES, 8)
     for side in range(2):
@@ -235,9 +254,16 @@
             ar[base : base + BNDS, :] = got[j * BNDS : (j + 1) * BNDS].astype(BF)
     degree = degree + nt(es1[4 * HUBS : 4 * HUBS + 16, :], ed1[...])[0:1]
     scale = 1.0 / jnp.maximum(degree, 1.0)
-    low_y = (yz[0:W] - high.astype(F32)).astype(BF)
-    near = nn(jnp.concatenate([high, low_y], axis=0), al[...])
-    pooled = near[0:W] + near[W : 2 * W]
+    diag = lax.broadcasted_iota(jnp.int32, (W, W), 0) == lax.broadcasted_iota(jnp.int32, (W, W), 1)
+    bias = jnp.sum(jnp.where(diag, b_v[...].astype(F32), 0.0), axis=1, keepdims=True)
+    eye = jnp.where(
+        lax.broadcasted_iota(jnp.int32, (128, 128), 0)
+        == lax.broadcasted_iota(jnp.int32, (128, 128), 1), 1.0, 0.0,
+    ).astype(BF)
+
+    pooled = nn(own, al[...])
+    all_of(others, y_recv.at[0]).wait()
+    own_term = nn(w_v[:, 0:256], xg[...].reshape(NY * W, NODES)) + bias
 
     def add_half(side):
         rows = recv[side].reshape(ROWS, 128)
@@ -251,26 +277,30 @@
         src_ref=recv.at[core], dst_ref=recv.at[core], send_sem=c_send, recv_sem=c_recv,
         device_id=sibling, device_id_type=MESH,
     )
-    pl.when(z >= DIRECT)(swap.start)
+    pl.when(z >= EARLY)(swap.start)
     pooled = pooled + add_half(core)
 
-    @pl.when(z >= DIRECT)
+    @pl.when(z >= EARLY)
     def _():
         swap.wait_recv()
 
-    @pl.when(z < DIRECT)
+    @pl.when(z < EARLY)
     def _():
         all_of(recv.at[0], d_recv.at[1]).wait()
 
     pooled = pooled + add_half(other)
 
-    out = yz[W : 2 * W] + bias + pooled * scale
+    ng[f] = (pooled * scale).astype(BF)
+    to_peers(ng, 1)
+    all_of(others, y_recv.at[1]).wait()
+    out = own_term + nn(w_v[:, 256:512], ng[...].reshape(NY * W, NODES))
     o_ref[...] = jnp.maximum(out, 0.0).astype(BF)
-    all_of(others, y_send).wait()
+    all_of(others, y_send.at[0]).wait()
+    all_of(others, y_send.at[1]).wait()
     all_of(rest, d_send.at[0]).wait()
-    all_of(recv.at[0, pl.ds(0, NX * DIRECT)], d_send.at[1]).wait()
-
-    @pl.when(z >= DIRECT)
+    all_of(recv.at[0, pl.ds(0, NX * EARLY)], d_send.at[1]).wait()
+
+    @pl.when(z >= EARLY)
     def _():
         swap.wait_send()
 
@@ -291,12 +321,12 @@
         scratch_shapes=[
             V((W, NODES), BF), V((1, W), BF), V((16, 128), I32), V((16, 128), I32),
             V((1, 16), I32), V((16, 128), I32), V((16, 128), I32), V((8, 96), I32),
-            V((NY, W, NODES), BF), V((NODES, 1024), BF),
+            V((NY, W, NODES), BF), V((NY, W, NODES), BF), V((NODES, 1024), BF),
             V((NODES, EDGES), BF), V((NODES + 16, EDGES), BF),
             V((NODES, EDGES // 2), BF), V((4 * HUBS + 16, EDGES // 2), BF),
             V((NODES, NODES), BF), V((8 * LINES, NODES), BF), V((ROWS, 256), BF),
             V((ROWS, LINES), BF), V((NQ, 8, 128), BF), V((2, NQ, 8, 128), BF),
-            DMA((11,)), REGULAR, REGULAR, DMA(()), DMA(()), DMA((2,)), DMA((2,)),
+            DMA((11,)), REGULAR, REGULAR, REGULAR, DMA((2,)), DMA((2,)), DMA((2,)), DMA((2,)),
             DMA(()), DMA(()),
         ],
         compiler_params=pltpu.CompilerParams(

time: 36.8 us -> 37 us (level)
  the two profiles are of different devices: /device:TPU:193 before, /device:TPU:513 now
where the time goes in v6:
time: 37 us; the launch traced here: 36.8 us
  Pallas kernels  35.4 us (96%)
  local copies, waits for them, and re-layouts  1.38 us (4%)
    pallas_call x1, Pallas kernels, shards(): pl.pallas_call(kernel, out_shape=jax.ShapeDtypeStruct((W, NODES), BF), in...  35.4 us
    unnamed x1, local copies, waits for them, and re-layouts  1.38 us

profile of v6, /device:TPU:513, one launch (start us, length us, event | category | flops | bytes accessed | tf_op | source)
XLA Modules:
  0.0 36.8 jit_solution(7638321399884354876)
XLA Ops:
  0.0 35.4 %shard_map.109 = bf16[32,512]{1,0:T(8,128)(2,1)} custom-call(bf16[32,512]{1,0:T(8,128)(2,1)} %bitcast.13, bf16[32,512]{1,0:T(8,128)(2,1)} %bitcast.14, bf16[1,32]{1,0:T(2,128)(2,1)} %bitcast.22, s32[16,128]{1,0:T(8,128)} %bitcast.15, s32[16,128]{1,0:T(8,128)} %bitcast.16, s32[1,16]{1,0:T(1,128)} %bitcast.23, s32[8,128]{1,0:T(8,128)} %bitcast.17, ...), custom_call_target="tpu_custom_call" | custom-call | tf_op jit(solution)/shard_map/pallas_call | solution.py:316
  35.4 1.4 %copy.13 = bf16[512,32]{0,1:T(8,128)(2,1)} copy(bf16[512,32]{0,1:T(8,128)(2,1)} %bitcast.12) | data formatting | bytes 65536

commit v7 on v6

--- a/solution.py
+++ b/solution.py
@@ -18,7 +18,8 @@
 BNDS = NQ * 2
 LINES = HUBS + BNDS
 EARLY = 6
-Y_ORDER = (4, 3, 5, 2, 6, 1, 7)
+DIRECT = 3
+Y_ORDER = (4, 5, 3, 6, 2, 7, 1)
 
 
 def nt(a, b):
@@ -92,14 +93,19 @@
                 for on in range(2):
                     signal(barrier, chip(xx, zz, on))
 
-    for copy in loads:
-        copy.wait()
-
     lane = lax.broadcasted_iota(jnp.int32, (16, 512), 1)
     hub = lax.broadcasted_iota(jnp.int32, (16, 512), 0)
     spread = jnp.where(
         (lane // 128 == hub % 4) & (lane % 128 == 96 + hub // 4), 1.0, 0.0
     ).astype(BF)
+    row = lax.broadcasted_iota(jnp.int32, (ROWS, 256), 0)
+    col = lax.broadcasted_iota(jnp.int32, (ROWS, 256), 1)
+    t = row % 8
+    want = jnp.where(t < 4, (t % 2) * 128 + (row // 8) * 2 + t // 2, 92 + t)
+    pick[...] = jnp.where(col == want, 1.0, 0.0).astype(BF)
+    for copy in loads[:3]:
+        copy.wait()
+
     hub_lanes = nn(one_hot(hr_v[...], NODES), spread)
     for c in range(8):
         part = one_hot(sr_v[c : c + 1, :], NODES)
@@ -108,16 +114,13 @@
         if si == 0:
             part = part + hub_lanes[:, j * 128 : j * 128 + 128].astype(BF)
         ot[:, j * 256 + si * 128 : j * 256 + si * 128 + 128] = part
-    row = lax.broadcasted_iota(jnp.int32, (ROWS, 256), 0)
-    col = lax.broadcasted_iota(jnp.int32, (ROWS, 256), 1)
-    t = row % 8
-    want = jnp.where(t < 4, (t % 2) * 128 + (row // 8) * 2 + t // 2, 92 + t)
-    pick[...] = jnp.where(col == want, 1.0, 0.0).astype(BF)
-    line = lax.broadcasted_iota(jnp.int32, (ROWS, LINES), 0)
-    at = lax.broadcasted_iota(jnp.int32, (ROWS, LINES), 1)
-    low = at - HUBS
-    want = jnp.where(low < 0, (at // 4) * 8 + 4 + at % 4, (low // 2) * 8 + 2 * core + low % 2)
-    sel[...] = jnp.where(line == want, 1.0, 0.0).astype(BF)
+
+    pl.semaphore_wait(barrier, rank + 2 * NX - 1 + 2 * NX * jnp.minimum(z, EARLY))
+
+    @pl.when(z > 0)
+    def _():
+        for xx in range(NX):
+            signal(heard.at[z], chip(xx, 0))
 
     def all_of(region, sem):
         return pltpu.make_async_copy(region, region, sem)
@@ -150,15 +153,11 @@
 
     def send_early_plane(zz):
         send_plane(zz)
-        for xx in range(NX):
-            send_across(xx, zz)
-
-    pl.semaphore_wait(barrier, rank + 2 * NX - 1 + 2 * NX * jnp.minimum(z, EARLY))
-
-    @pl.when(z > 0)
-    def _():
-        for xx in range(NX):
-            signal(heard, chip(xx, 0))
+
+        @pl.when(zz < DIRECT)
+        def _():
+            for xx in range(NX):
+                send_across(xx, zz)
 
     pl.loop(0, jnp.minimum(z + 1, EARLY))(send_early_plane)
 
@@ -172,6 +171,8 @@
         signal(ready, at_rank(r))
 
     recv[core, q] = sendb[q]
+    for copy in loads[3:]:
+        copy.wait()
 
     def hot_rows(ref, at, out, size, first=0):
         @pl.loop(0, out.shape[1] // 128)
@@ -201,6 +202,22 @@
         pl.semaphore_wait(ready, NY - 1 - rank)
 
     to_peers(xg, 0)
+
+    def send_late_plane(zz):
+        for xx in range(NX):
+            send_rows_to(xx, zz)
+
+    @pl.when(z >= EARLY)
+    def _():
+        pl.semaphore_wait(all_in, 1)
+        pl.loop(EARLY, z)(send_late_plane)
+        pl.loop(z + 1, NZ)(send_late_plane)
+
+    line = lax.broadcasted_iota(jnp.int32, (ROWS, LINES), 0)
+    at = lax.broadcasted_iota(jnp.int32, (ROWS, LINES), 1)
+    low = at - HUBS
+    want = jnp.where(low < 0, (at // 4) * 8 + 4 + at % 4, (low // 2) * 8 + 2 * core + low % 2)
+    sel[...] = jnp.where(line == want, 1.0, 0.0).astype(BF)
 
     h = es_v[0:8, :]
     s = h // 16
@@ -219,7 +236,17 @@
     degree = degree + got[4 * HUBS : 4 * HUBS + 1]
     @pl.when(z == 0)
     def _():
-        pl.semaphore_wait(heard, NX * (NZ - 1))
+        @pl.loop(1, NZ)
+        def _(zz):
+            pl.semaphore_wait(heard.at[zz], NX)
+
+            @pl.when(zz < EARLY)
+            def _():
+                send_early_plane(zz)
+
+            @pl.when(zz >= EARLY)
+            def _():
+                send_late_plane(zz)
 
         @pl.when(x > 0)
         def _():
@@ -231,19 +258,6 @@
                 @pl.when(x == 1)
                 def _():
                     signal(all_in, chip(0, zz))
-
-    @pl.when(z > 0)
-    def _():
-        pl.semaphore_wait(all_in, 1)
-
-    pl.loop(jnp.minimum(z + 1, EARLY), EARLY)(send_early_plane)
-
-    @pl.loop(EARLY, NZ)
-    def _(zz):
-        @pl.when(zz != z)
-        def _():
-            for xx in range(NX):
-                send_rows_to(xx, zz)
 
     hot_rows(ed_v, 0, ed1, NODES, 8)
     for side in range(2):
@@ -254,6 +268,13 @@
             ar[base : base + BNDS, :] = got[j * BNDS : (j + 1) * BNDS].astype(BF)
     degree = degree + nt(es1[4 * HUBS : 4 * HUBS + 16, :], ed1[...])[0:1]
     scale = 1.0 / jnp.maximum(degree, 1.0)
+
+    @pl.when((z > 0) & (z < EARLY))
+    def _():
+        pl.semaphore_wait(all_in, 1)
+        pl.loop(z + 1, EARLY)(send_early_plane)
+        pl.loop(EARLY, NZ)(send_late_plane)
+
     diag = lax.broadcasted_iota(jnp.int32, (W, W), 0) == lax.broadcasted_iota(jnp.int32, (W, W), 1)
     bias = jnp.sum(jnp.where(diag, b_v[...].astype(F32), 0.0), axis=1, keepdims=True)
     eye = jnp.where(
@@ -277,14 +298,14 @@
         src_ref=recv.at[core], dst_ref=recv.at[core], send_sem=c_send, recv_sem=c_recv,
         device_id=sibling, device_id_type=MESH,
     )
-    pl.when(z >= EARLY)(swap.start)
+    pl.when(z >= DIRECT)(swap.start)
     pooled = pooled + add_half(core)
 
-    @pl.when(z >= EARLY)
+    @pl.when(z >= DIRECT)
     def _():
         swap.wait_recv()
 
-    @pl.when(z < EARLY)
+    @pl.when(z < DIRECT)
     def _():
         all_of(recv.at[0], d_recv.at[1]).wait()
 
@@ -298,9 +319,9 @@
     all_of(others, y_send.at[0]).wait()
     all_of(others, y_send.at[1]).wait()
     all_of(rest, d_send.at[0]).wait()
-    all_of(recv.at[0, pl.ds(0, NX * EARLY)], d_send.at[1]).wait()
-
-    @pl.when(z >= EARLY)
+    all_of(recv.at[0, pl.ds(0, NX * DIRECT)], d_send.at[1]).wait()
+
+    @pl.when(z >= DIRECT)
     def _():
         swap.wait_send()
 
@@ -326,7 +347,7 @@
             V((NODES, EDGES // 2), BF), V((4 * HUBS + 16, EDGES // 2), BF),
             V((NODES, NODES), BF), V((8 * LINES, NODES), BF), V((ROWS, 256), BF),
             V((ROWS, LINES), BF), V((NQ, 8, 128), BF), V((2, NQ, 8, 128), BF),
-            DMA((11,)), REGULAR, REGULAR, REGULAR, DMA((2,)), DMA((2,)), DMA((2,)), DMA((2,)),
+            DMA((11,)), REGULAR, REGULAR((NZ,)), REGULAR, DMA((2,)), DMA((2,)), DMA((2,)), DMA((2,)),
             DMA(()), DMA(()),
         ],
         compiler_params=pltpu.CompilerParams(

time: 37 us -> 36.4 us (0.984)
  the two profiles are of different devices: /device:TPU:513 before, /device:TPU:193 now
where the time goes in v7:
time: 36.4 us; the launch traced here: 36.2 us
  Pallas kernels  34.8 us (96%)
  local copies, waits for them, and re-layouts  1.38 us (4%)
    pallas_call x1, Pallas kernels, shards(): pl.pallas_call(kernel, out_shape=jax.ShapeDtypeStruct((W, NODES), BF), in...  34.8 us
    unnamed x1, local copies, waits for them, and re-layouts  1.38 us

profile of v7, /device:TPU:193, one launch (start us, length us, event | category | flops | bytes accessed | tf_op | source)
XLA Modules:
  0.0 36.2 jit_solution(11811953152677167825)
XLA Ops:
  0.0 34.8 %shard_map.109 = bf16[32,512]{1,0:T(8,128)(2,1)} custom-call(bf16[32,512]{1,0:T(8,128)(2,1)} %bitcast.13, bf16[32,512]{1,0:T(8,128)(2,1)} %bitcast.14, bf16[1,32]{1,0:T(2,128)(2,1)} %bitcast.22, s32[16,128]{1,0:T(8,128)} %bitcast.15, s32[16,128]{1,0:T(8,128)} %bitcast.16, s32[1,16]{1,0:T(1,128)} %bitcast.23, s32[8,128]{1,0:T(8,128)} %bitcast.17, ...), custom_call_target="tpu_custom_call" | custom-call | tf_op jit(solution)/shard_map/pallas_call | solution.py:337
  34.8 1.4 %copy.13 = bf16[512,32]{0,1:T(8,128)(2,1)} copy(bf16[512,32]{0,1:T(8,128)(2,1)} %bitcast.12) | data formatting | bytes 65536

commit v8 on v7

--- a/solution.py
+++ b/solution.py
@@ -277,10 +277,6 @@
 
     diag = lax.broadcasted_iota(jnp.int32, (W, W), 0) == lax.broadcasted_iota(jnp.int32, (W, W), 1)
     bias = jnp.sum(jnp.where(diag, b_v[...].astype(F32), 0.0), axis=1, keepdims=True)
-    eye = jnp.where(
-        lax.broadcasted_iota(jnp.int32, (128, 128), 0)
-        == lax.broadcasted_iota(jnp.int32, (128, 128), 1), 1.0, 0.0,
-    ).astype(BF)
 
     pooled = nn(own, al[...])
     all_of(others, y_recv.at[0]).wait()
@@ -288,7 +284,9 @@
 
     def add_half(side):
         rows = recv[side].reshape(ROWS, 128)
-        turned = nn(nt(eye, rows).astype(BF), sel[...]).astype(BF)
+        turned = lax.dot_general(
+            rows, sel[...], (((0,), (0,)), ((), ())), preferred_element_type=F32
+        ).astype(BF)
         wide = jnp.concatenate([turned[j * W : j * W + W] for j in range(4)], axis=1)
         return nn(wide, ar[pl.ds(pl.multiple_of(side * (4 * LINES), 16), 4 * LINES), :])
 

time: 36.4 us -> 36.3 us (level)
  no operation moved by 1% of the time
where the time goes in v8:
time: 36.3 us; the launch traced here: 36 us
  Pallas kernels  34.6 us (95%)
  local copies, waits for them, and re-layouts  1.38 us (4%)
    pallas_call x1, Pallas kernels, shards(): pl.pallas_call(kernel, out_shape=jax.ShapeDtypeStruct((W, NODES), BF), in...  34.6 us
    unnamed x1, local copies, waits for them, and re-layouts  1.38 us

profile of v8, /device:TPU:193, one launch (start us, length us, event | category | flops | bytes accessed | tf_op | source)
XLA Modules:
  0.0 36.0 jit_solution(10584382309913275038)
XLA Ops:
  0.0 34.6 %shard_map.109 = bf16[32,512]{1,0:T(8,128)(2,1)} custom-call(bf16[32,512]{1,0:T(8,128)(2,1)} %bitcast.13, bf16[32,512]{1,0:T(8,128)(2,1)} %bitcast.14, bf16[1,32]{1,0:T(2,128)(2,1)} %bitcast.22, s32[16,128]{1,0:T(8,128)} %bitcast.15, s32[16,128]{1,0:T(8,128)} %bitcast.16, s32[1,16]{1,0:T(1,128)} %bitcast.23, s32[8,128]{1,0:T(8,128)} %bitcast.17, ...), custom_call_target="tpu_custom_call" | custom-call | tf_op jit(solution)/shard_map/pallas_call | solution.py:335
  34.7 1.4 %copy.13 = bf16[512,32]{0,1:T(8,128)(2,1)} copy(bf16[512,32]{0,1:T(8,128)(2,1)} %bitcast.12) | data formatting | bytes 65536
